TPU v7x, 256 devices: a whole 4x4x8 slice. The times are simulated.
256 devices in a mesh: seq: 16 (over z_lo, y), head: 16 (over x, z_hi, core).
Axes of the slice: x: 4, y: 4, z: 8 (z_hi: 2, z_lo: 4; z = z_hi * 4 + z_lo), core: 2. Of those that a mesh axis runs over, the one named last changes fastest.
Arguments:
- queries: bfloat16 [8192, 4096], P('seq', 'head'), may hold values from -60 to 60
- keys: bfloat16 [8192, 4096], P('seq', 'head'), may hold values from -60 to 60
- values: bfloat16 [8192, 4096], P('seq', 'head'), may hold values from -6 to 6
- w_out: bfloat16 [4096, 4096], P('head'), may hold values from -0.125 to 0.125
- d_mixed: bfloat16 [8192, 4096], P('seq', 'head'), may hold values from -6 to 6
- random_blocks: int32 [64, 3], P('seq'), may hold values from 0 to 63, as said below
- global_blocks: int32 [2], replicated, may hold values from 0 to 63, as said below
Outputs:
- mixed: bfloat16 [8192, 4096], P('seq', 'head')
- query_grad: bfloat16 [8192, 4096], P('seq', 'head')
- key_grad: bfloat16 [8192, 4096], P('seq', 'head')
- value_grad: bfloat16 [8192, 4096], P('seq', 'head')
Inputs may be any that keep to these rules, and one draw needn't show every extreme that they name: `random_blocks`: blocks b * 4 to (b + 1) * 4 - 1 lie on index b of seq. The random blocks named by the 4 query blocks of one index of seq include at most 2 distinct blocks of any one index of seq, and exactly 2 for some. `global_blocks`: the 2 global blocks are distinct; the document's last block is always one of them.
All inputs are finite; a program needn't handle non-finite values.
Results may differ from a plain program's by a relative error of at most 0.033.
Values may be sent and summed in bfloat16 or wider, within the bound.
A program may use at most 128 MiB of HBM per device.

v0:
```python
from functools import partial

import jax
import jax.numpy as jnp
from jax import lax
from jax.sharding import PartitionSpec as P

HEAD_DIM = 128
BLOCK = 128


def slot_table(first_ids, block_count, random_rows, global_blocks):
    band_ids = first_ids[:, None] + jnp.arange(-1, 2, dtype=jnp.int32)[None, :]
    global_ids = jnp.broadcast_to(
        global_blocks[None, :], (first_ids.shape[0], global_blocks.shape[0])
    )
    slot_ids = jnp.concatenate([band_ids, random_rows, global_ids], axis=1)
    inside = (slot_ids >= 0) & (slot_ids < block_count)
    slot_count = slot_ids.shape[1]
    same_block = slot_ids[:, :, None] == slot_ids[:, None, :]
    earlier = jnp.arange(slot_count)[None, :] < jnp.arange(slot_count)[:, None]
    repeated = jnp.any(same_block & earlier[None, :, :], axis=2)
    return (slot_ids, inside & jnp.logical_not(repeated))


def body(queries, keys, values, w_out, d_mixed, random_blocks, global_blocks):
    row_count, features = queries.shape
    blocks_here = row_count // BLOCK
    heads_here = features // HEAD_DIM
    shards = lax.axis_size("seq")
    block_count = blocks_here * shards
    my_index = lax.axis_index("seq")
    first_block = my_index * blocks_here
    score_scale = HEAD_DIM ** (-0.5)
    own_ids = first_block + jnp.arange(blocks_here, dtype=jnp.int32)
    slot_ids, slot_live = slot_table(own_ids, block_count, random_blocks, global_blocks)
    slot_count = slot_ids.shape[1]
    key_values = jnp.concatenate([keys, values], axis=1)
    blank_blocks = jnp.zeros(slot_ids.shape + (BLOCK, 2 * features), jnp.bfloat16)
    shard_rows = lax.all_gather(key_values, "seq", axis=0, tiled=True)
    piece_rows = shard_rows.shape[0]
    local_rows = slot_ids[:, :, None] * BLOCK + jnp.arange(BLOCK, dtype=jnp.int32)[None, None, :]
    inside = (local_rows >= 0) & (local_rows < piece_rows)
    picked = shard_rows[jnp.clip(local_rows, 0, piece_rows - 1)]
    fetched = jnp.where(inside[..., None], picked, blank_blocks)
    kv_rows = fetched.reshape(blocks_here, slot_count * BLOCK, 2 * features)
    key_heads = kv_rows[:, :, :features].reshape(
        blocks_here, slot_count * BLOCK, heads_here, HEAD_DIM
    )
    value_heads = kv_rows[:, :, features:].reshape(
        blocks_here, slot_count * BLOCK, heads_here, HEAD_DIM
    )
    query_heads = queries.reshape(blocks_here, BLOCK, heads_here, HEAD_DIM)
    row_mask = jnp.repeat(slot_live, BLOCK, axis=1)
    logits = (
        jnp.einsum("qihd,qkhd->qhik", query_heads, key_heads, preferred_element_type=jnp.float32)
        * score_scale
    )
    logits = jnp.where(row_mask[:, None, None, :], logits, -1e30)
    row_max = jnp.max(logits, axis=-1, keepdims=True)
    log_total = row_max + jnp.log(jnp.sum(jnp.exp(logits - row_max), axis=-1, keepdims=True))
    prob_full = jnp.exp(logits - log_total)
    prob_half = prob_full.astype(jnp.bfloat16)
    attended = jnp.einsum(
        "qhik,qkhd->qihd", prob_half, value_heads, preferred_element_type=jnp.float32
    )
    attended = attended.astype(jnp.bfloat16).reshape(row_count, features)
    head_terms = jnp.dot(attended, w_out, preferred_element_type=jnp.float32)
    mixed = lax.psum_scatter(
        head_terms.astype(jnp.bfloat16), "head", scatter_dimension=1, tiled=True
    )
    full_grad = lax.all_gather(d_mixed, "head", axis=1, tiled=True)
    d_attn = lax.dot_general(
        full_grad, w_out, (((1,), (1,)), ((), ())), preferred_element_type=jnp.float32
    ).astype(jnp.bfloat16)
    row_deltas = jnp.sum(
        (attended.astype(jnp.float32) * d_attn.astype(jnp.float32)).reshape(
            row_count, heads_here, HEAD_DIM
        ),
        axis=-1,
    )
    delta_heads = jnp.transpose(row_deltas.reshape(blocks_here, BLOCK, heads_here), (0, 2, 1))
    grad_heads = d_attn.reshape(blocks_here, BLOCK, heads_here, HEAD_DIM)
    prob_grad = jnp.einsum(
        "qihd,qkhd->qhik", grad_heads, value_heads, preferred_element_type=jnp.float32
    )
    score_grad = (prob_full * (prob_grad - delta_heads[..., None]) * score_scale).astype(
        jnp.bfloat16
    )
    query_grad = jnp.einsum(
        "qhik,qkhd->qihd", score_grad, key_heads, preferred_element_type=jnp.float32
    )
    query_grad = query_grad.astype(jnp.bfloat16).reshape(row_count, features)
    row_totals = jnp.transpose(log_total[..., 0], (0, 2, 1)).reshape(row_count, heads_here)
    attends = jnp.any(
        (slot_ids[:, :, None] == jnp.arange(block_count, dtype=jnp.int32)[None, None, :])
        & slot_live[:, :, None],
        axis=1,
    ).astype(jnp.float32)
    all_totals, all_deltas, all_attends = (
        lax.all_gather(row_totals, "seq", axis=0, tiled=True),
        lax.all_gather(row_deltas, "seq", axis=0, tiled=True),
        lax.all_gather(attends, "seq", axis=0, tiled=True),
    )
    own_keys = keys.reshape(blocks_here, BLOCK, heads_here, HEAD_DIM)
    own_values = values.reshape(blocks_here, BLOCK, heads_here, HEAD_DIM)
    blank_pair = jnp.zeros((BLOCK, heads_here, HEAD_DIM), jnp.float32)

    def pair_terms(key_index, query_block, grad_block, totals, deltas):
        pair_logits = (
            jnp.einsum(
                "ihd,khd->hik", query_block, own_keys[key_index], preferred_element_type=jnp.float32
            )
            * score_scale
        )
        pair_prob = jnp.exp(pair_logits - totals[..., None])
        pair_grad = jnp.einsum(
            "ihd,khd->hik", grad_block, own_values[key_index], preferred_element_type=jnp.float32
        )
        pair_score = (pair_prob * (pair_grad - deltas[..., None]) * score_scale).astype(
            jnp.bfloat16
        )
        key_add = jnp.einsum(
            "hik,ihd->khd", pair_score, query_block, preferred_element_type=jnp.float32
        )
        value_add = jnp.einsum(
            "hik,ihd->khd",
            pair_prob.astype(jnp.bfloat16),
            grad_block,
            preferred_element_type=jnp.float32,
        )
        return (key_add, value_add)

    def no_terms():
        return (blank_pair, blank_pair)

    blank_sums = jnp.zeros((blocks_here, BLOCK, heads_here, HEAD_DIM), jnp.float32)
    query_rows = lax.all_gather(queries, "seq", axis=0, tiled=True)
    grad_rows = lax.all_gather(d_attn, "seq", axis=0, tiled=True)
    piece_blocks = query_rows.shape[0] // BLOCK

    def one_block(block_index, inner):
        key_sum, value_sum = inner
        row_start = block_index * BLOCK
        query_block = lax.dynamic_slice_in_dim(query_rows, row_start, BLOCK, 0).reshape(
            BLOCK, heads_here, HEAD_DIM
        )
        grad_block = lax.dynamic_slice_in_dim(grad_rows, row_start, BLOCK, 0).reshape(
            BLOCK, heads_here, HEAD_DIM
        )
        totals = jnp.transpose(lax.dynamic_slice_in_dim(all_totals, row_start, BLOCK, 0))
        deltas = jnp.transpose(lax.dynamic_slice_in_dim(all_deltas, row_start, BLOCK, 0))
        wanted = lax.dynamic_slice_in_dim(all_attends, row_start // BLOCK, 1, 0)[0]
        for key_index in range(blocks_here):
            member = (
                lax.dynamic_index_in_dim(wanted, first_block + key_index, 0, keepdims=False) > 0.5
            )
            compute = partial(pair_terms, key_index, query_block, grad_block, totals, deltas)
            key_add, value_add = lax.cond(member, compute, no_terms)
            key_sum = key_sum.at[key_index].add(key_add)
            value_sum = value_sum.at[key_index].add(value_add)
        return (key_sum, value_sum)

    key_sum, value_sum = lax.fori_loop(0, piece_blocks, one_block, (blank_sums, blank_sums))
    key_grad = key_sum.reshape(row_count, features).astype(jnp.bfloat16)
    value_grad = value_sum.reshape(row_count, features).astype(jnp.bfloat16)
    return (mixed, query_grad, key_grad, value_grad)


def solution(mesh):
    return jax.shard_map(
        body,
        mesh=mesh,
        in_specs=(
            P("seq", "head"),
            P("seq", "head"),
            P("seq", "head"),
            P("head", None),
            P("seq", "head"),
            P("seq", None),
            P(),
        ),
        out_specs=(P("seq", "head"), P("seq", "head"), P("seq", "head"), P("seq", "head")),
        check_vma=False,
    )
```

profile of v0, /device:TPU:82, one launch (start us, length us, event | category | flops | bytes accessed | tf_op | source)
XLA Modules:
  0.0 1466.2 jit_solution(16100717372649321060)
XLA Ops:
  15.0 94.8 %all-gather.6.cloned.1.call-done = bf16[8192,512]{1,0:T(8,128)(2,1)} async-done(((bf16[512,512]{1,0:T(8,128)(2,1)}), bf16[8192,512]{1,0:T(8,128)(2,1)}) %all-gather.6.cloned.1.call-update) | async-done | bytes 8388624 | tf_op jit(solution)/shard_map/all_gather | solution.py:40
  109.8 21.8 %gather_fusion = bf16[4096,512]{1,0:T(8,128)(2,1)} fusion(bf16[8192,512]{1,0:T(8,128)(2,1)} %all-gather.6.cloned.1.call-done, s32[4096]{0:T(1024)S(1)} %fusion.92), kind=kCustom, calls=%fused_computation | custom fusion | bytes 8404992 | tf_op jit(solution)/shard_map/gather | solution.py:44
  131.7 6.3 copy.138
  147.2 42.3 %all-gather.8.cloned.1.call-done = bf16[512,4096]{1,0:T(8,128)(2,1)} async-done(((bf16[512,256]{1,0:T(8,128)(2,1)}), bf16[512,4096]{1,0:T(8,128)(2,1)}) %all-gather.8.cloned.1.call-update) | async-done | bytes 4194320 | tf_op jit(solution)/shard_map/all_gather | solution.py:72
  189.5 4.2 bitcast_reduce_fusion.1
  195.5 32.9 %all-gather = f32[16,4,64]{2,1,0:T(4,128)} all-gather(f32[1,4,64]{2,1,0:T(4,128)S(1)} %convert_bitcast_fusion), channel_id=1, replica_groups=mesh['seq'=16,'head'=16] {'seq'}, dimensions={0}, use_global_device_ids=true | all-gather | bytes 17408 | tf_op jit(solution)/shard_map/all_gather | solution.py:103
  229.4 6.0 fusion.86
  236.3 40.0 %all_gather.27 = f32[8192,2]{0,1:T(2,128)} all-gather(f32[512,2]{0,1:T(2,128)S(1)} %get-tuple-element.915), channel_id=1, replica_groups=mesh['seq'=16,'head'=16] {'seq'}, dimensions={0}, use_global_device_ids=true | all-gather | bytes 69632 | tf_op jit(solution)/shard_map/all_gather | solution.py:102
  276.3 39.5 %all_gather.25 = f32[8192,2]{0,1:T(2,128)} all-gather(f32[512,2]{0,1:T(2,128)S(1)} %bitcast.221), channel_id=1, replica_groups=mesh['seq'=16,'head'=16] {'seq'}, dimensions={0}, use_global_device_ids=true | all-gather | bytes 69632 | tf_op jit(solution)/shard_map/all_gather | solution.py:101
  315.8 3.2 convolution_convert_fusion
  319.1 41.1 %all-gather.12.cloned.1.call-done = bf16[8192,256]{0,1:T(8,128)(2,1)} async-done(((bf16[512,256]{0,1:T(8,128)(2,1)}), bf16[8192,256]{0,1:T(8,128)(2,1)}) %all-gather.12.cloned.1.call-update) | async-done | bytes 4194320 | tf_op jit(solution)/shard_map/all_gather | solution.py:139
  360.3 1097.8 %while.26 = (s32[]{:T(128)}, f32[4,128,2,128]{3,1,2,0:T(8,128)S(1)}, f32[4,128,2,128]{3,1,2,0:T(8,128)S(1)}, f32[64,64]{1,0:T(8,128)}, s32[]{:T(128)}, /*index=5...) while((s32[]{:T(128)}, ...), condition=%wide.region_15.16_spmd, body=%wide.region_6.15_spmd.sunk | while | flops 135397408 | bytes 7615302 | solution.py:164
  371.7 3.2 conditional.10
  390.6 3.2 conditional.10
  407.0 3.2 conditional.10
  442.2 3.2 conditional.10
  457.1 3.2 conditional.9
  461.0 3.2 conditional.10
  477.4 3.2 conditional.10
  493.8 3.2 conditional.10
  575.4 3.2 conditional.10
  591.7 3.2 conditional.10
  640.7 3.2 conditional.10
  771.2 3.2 conditional.10
  893.1 3.2 conditional.10
  1109.1 3.2 conditional.10
  1128.0 3.2 conditional.10
  1212.0 3.2 conditional.10
  1228.3 3.2 conditional.10
  1261.0 3.2 conditional.10
  1293.6 3.2 conditional.10
  1450.7 3.2 conditional.10
  (1667 shorter events, 1269.4 us)
Async XLA Ops:
  7.2 182.3 %copy-start = (bf16[256,4096]{1,0:T(8,128)(2,1)S(1)}, bf16[256,4096]{1,0:T(8,128)(2,1)}, u32[]{:S(2)}) copy-start(bf16[256,4096]{1,0:T(8,128)(2,1)} %param.36) | copy-start | bytes 6291460
  7.2 102.6 %all-gather.6.cloned.1.call-start = ((), (), s32[]{:S(2)}) async-start(), calls=%async_computation.1 | async-start | bytes 8912896 | tf_op jit(solution)/shard_map/all_gather | solution.py:40
  9.3 180.2 %all-gather.8.cloned.1.call-start = ((), (), s32[]{:S(2)}) async-start(), calls=%async_computation.3 | async-start | bytes 4456448 | tf_op jit(solution)/shard_map/all_gather | solution.py:72
  10.0 309.1 %all-gather.10.cloned.1.call-start = ((), (), s32[]{:S(2)}) async-start(), calls=%async_computation.4 | async-start | bytes 4456448 | tf_op jit(solution)/shard_map/all_gather | solution.py:138
  11.9 348.3 %all-gather.12.cloned.1.call-start = ((), (), s32[]{:S(2)}) async-start(), calls=%async_computation.5 | async-start | bytes 4456448 | tf_op jit(solution)/shard_map/all_gather | solution.py:139
  140.9 1.8 copy-start.2
  141.0 3.0 copy-start.3
  142.7 2.0 copy-start.1
  147.2 46.5 %copy-start.4 = (bf16[512,256]{1,0:T(8,128)(2,1)S(1)}, bf16[512,256]{1,0:T(8,128)(2,1)}, u32[]{:S(2)}) copy-start(bf16[512,256]{1,0:T(8,128)(2,1)} %param.34) | copy-start | bytes 786436
  147.2 46.6 %copy-start.5 = (bf16[512,256]{1,0:T(8,128)(2,1)S(1)}, bf16[512,256]{1,0:T(8,128)(2,1)}, u32[]{:S(2)}) copy-start(bf16[512,256]{1,0:T(8,128)(2,1)} %param.35) | copy-start | bytes 786436
  193.7 1266.0 %reduce-scatter.2.cloned.1.call-start = ((), (), s32[]{:S(2)}) async-start(), calls=%async_computation.2 | async-start | bytes 4456448 | tf_op jit(solution)/shard_map/reduce_scatter | solution.py:69
Sparse Core Ops, SparseCore 0:
  9.8 99.9 all-gather.5
  112.4 77.0 all-gather.7
  191.8 78.9 all-gather.9
  273.1 87.1 all-gather.11
  365.0 108.0 reduce-scatter.1
where the time goes:
time: 1490 us; the launch traced here: 1470 us
  local copies, waits for them, and re-layouts  441 us (30%)
  matrix products  289 us (19%)
  other arithmetic  253 us (17%)
  waiting for transfers between devices  179 us (12%)
  loops' own time  177 us (12%)
  blocking collectives  112 us (8%)
    scatter-add x256, other arithmetic, one_block(): value_sum = value_sum.at[key_index].add(value_add)  241 us
    another operation x1, loops' own time, body(): lax.fori_loop(0, piece_blocks, one_block, (blank_sums, blank_sums))  173 us
    another operation x342, local copies, waits for them, and re-layouts  115 us
    dot_general x85, matrix products, pair_terms(): jnp.einsum('hik,ihd->khd', pair_score, query_block, preferred_element_typ...  106 us
    dynamic_slice x64, local copies, waits for them, and re-layouts, one_block(): lax.dynamic_index_in_dim(wanted, first_block + key_index, 0, keepdims=False)  95.6 us
    all_gather x1, waiting for transfers between devices, body(): shard_rows = lax.all_gather(key_values, 'seq', axis=0, tiled=True)  94.8 us
    dot_general x85, matrix products, pair_terms(): jnp.einsum('ihd,khd->hik', query_block, own_keys[key_index], preferred_el...  90.6 us
    dot_general x85, matrix products, pair_terms(): jnp.einsum('hik,ihd->khd', pair_prob.astype(jnp.bfloat16), grad_block, pr...  75.1 us
  transfers between devices with their start and end apart: 5, of which 3 were waited for; matrix products, arithmetic and copies ran while one was open for 67% of the time, Pallas kernels for 0%

commit v1 on v0

v1 whole, which is shorter than its diff:
```python
import jax
import jax.numpy as jnp
from jax import lax
from jax.experimental import pallas as pl
from jax.experimental.pallas import tpu as pltpu
from jax.sharding import PartitionSpec as P

HEAD_DIM = 128
BLOCK = 128
SLOTS = 8
MASKED = -1e30
MESH = pl.DeviceIdType.MESH
BF16 = jnp.bfloat16
F32 = jnp.float32
VMEM_LIMIT = 56 * 1024 * 1024


def place():
    seq, head = lax.axis_index("seq"), lax.axis_index("head")
    return seq // 4, seq % 4, head // 4, (head // 2) % 2, head % 2


def dev(z, y, x, zh, core):
    return (z * 4 + y, x * 4 + zh * 2 + core)


def copy_to(src, dst, send_sem, recv_sem, device):
    return pltpu.make_async_remote_copy(
        src_ref=src,
        dst_ref=dst,
        send_sem=send_sem,
        recv_sem=recv_sem,
        device_id=device,
        device_id_type=MESH,
    )


def greet():
    z, y, x, zh, core = place()
    barrier = pltpu.get_barrier_semaphore()
    others = [dev(z, y, x, zh, 1 - core)]
    for step in (1, 2, 3):
        for r in (0, 1):
            others.append(dev((z + step) % 4, y, x, zh, r))
    others += [dev(z, (y + 1) % 4, x, zh, core), dev(z, (y + 3) % 4, x, zh, core)]
    others += [dev(z, y, (x + 1) % 4, zh, core), dev(z, y, (x + 3) % 4, zh, core)]
    others.append(dev(z, y, x, 1 - zh, core))
    for other in others:
        pl.semaphore_signal(barrier, inc=1, device_id=other, device_id_type=MESH)
    pl.semaphore_wait(barrier, len(others))


def gather_kernel(
    q_ref,
    k_ref,
    v_ref,
    dm_ref,
    w_ref,
    rb_ref,
    kv_ref,
    qm_ref,
    da_ref,
    rbm_ref,
    dm_all,
    grad,
    grad_acc,
    a_send,
    a_recv,
    b_send,
    b_recv,
    y_send,
    y_recv,
    ys_send,
    ys_recv,
    z_send,
    z_recv,
    x_send,
    x_recv,
    xs_send,
    xs_recv,
    g_send,
    g_recv,
):
    z, y, x, zh, core = place()
    sibling = dev(z, y, x, zh, 1 - core)
    sent = []
    greet()

    def send(src, dst, send_sem, recv_sem, device):
        copy = copy_to(src, dst, send_sem, recv_sem, device)
        copy.start()
        sent.append(copy)

    def arrive(dst, recv_sem, send_sem):
        copy_to(dst, dst, send_sem, recv_sem, sibling).wait_recv()

    y_up, y_down = dev(z, (y + 1) % 4, x, zh, core), dev(z, (y + 3) % 4, x, zh, core)
    x_up, x_down = dev(z, y, (x + 1) % 4, zh, core), dev(z, y, (x + 3) % 4, zh, core)
    y_of = {0: y, 1: (y + 3) % 4, 2: (y + 1) % 4, 3: (y + 2) % 4}
    x_of = {0: x, 1: (x + 3) % 4, 2: (x + 1) % 4, 3: (x + 2) % 4}

    own_dm = dm_all.at[core, x, zh]
    send(dm_ref, own_dm, z_send.at[0], z_recv.at[0], dev(z, y, x, 1 - zh, core))

    def to_line(src, dst, send_sem, recv_sem, j, r):
        there = 2 * core + j
        here = jnp.logical_and(there == z, core == r)

        @pl.when(here)
        def _():
            pltpu.make_async_copy(src, dst, recv_sem).start()

        @pl.when(jnp.logical_not(here))
        def _():
            copy_to(src, dst, send_sem, recv_sem, dev(there, y, x, zh, r)).start()

    def line_sent(src, dst, send_sem, recv_sem, j, r):
        there = 2 * core + j
        here = jnp.logical_and(there == z, core == r)

        @pl.when(jnp.logical_not(here))
        def _():
            copy_to(src, dst, send_sem, recv_sem, dev(there, y, x, zh, r)).wait_send()

    def line_args():
        for j in (0, 1):
            for r in (0, 1):
                rows, cols = pl.ds(r * 256, 256), pl.ds(j * 128, 128)
                for t, src in enumerate((k_ref, v_ref)):
                    yield (
                        src.at[rows, cols],
                        kv_ref.at[y, r, z, t],
                        a_send.at[t, j, r],
                        a_recv.at[t, z],
                        j,
                        r,
                    )
        for j in (0, 1):
            for r in (0, 1):
                rows, cols = pl.ds(r * 256, 256), pl.ds(j * 128, 128)
                yield (
                    q_ref.at[rows, cols],
                    qm_ref.at[z],
                    a_send.at[2, j, r],
                    a_recv.at[2, z],
                    j,
                    r,
                )

    for args in line_args():
        to_line(*args)
    send(dm_ref, own_dm, x_send.at[0, 0], x_recv.at[0, zh], x_up)
    send(dm_ref, own_dm, x_send.at[0, 1], x_recv.at[1, zh], x_down)
    send(dm_ref, own_dm, xs_send.at[0, 0], xs_recv.at[x, zh], sibling)
    for step in (1, 2, 3):
        send(
            rb_ref,
            rbm_ref.at[z],
            b_send.at[step - 1],
            b_recv.at[step - 1],
            dev((z + step) % 4, y, x, zh, core),
        )
    rbm_ref[z] = rb_ref[...]
    dm_all[core, x, zh] = dm_ref[...]

    for zz in range(4):
        for t in (0, 1):
            arrive(kv_ref.at[y, core, zz, t], a_recv.at[t, zz], a_send.at[t, 0, 0])
        piece = kv_ref.at[y, core, zz]
        send(piece, piece, y_send.at[0, zz], y_recv.at[0, zz], y_up)
        send(piece, piece, y_send.at[1, zz], y_recv.at[1, zz], y_down)
        send(piece, piece, ys_send.at[0, zz], ys_recv.at[0, zz], sibling)

    def dm_block(slot, k):
        return dm_all.at[core, x_of[slot], k]

    other_dm = dm_block(0, 1 - zh)
    arrive(other_dm, z_recv.at[0], z_send.at[0])
    send(other_dm, other_dm, x_send.at[1, 0], x_recv.at[0, 1 - zh], x_up)
    send(other_dm, other_dm, x_send.at[1, 1], x_recv.at[1, 1 - zh], x_down)
    send(other_dm, other_dm, xs_send.at[0, 1], xs_recv.at[x, 1 - zh], sibling)

    def kv_step(slot, recv, onward):
        for zz in range(4):
            piece = kv_ref.at[y_of[slot], core, zz]
            arrive(piece, recv(zz), y_send.at[0, zz])
            if zz in onward[0]:
                send(piece, piece, onward[1].at[zz], y_recv.at[2, zz], onward[2])
            send(piece, piece, ys_send.at[slot, zz], ys_recv.at[slot, zz], sibling)

    kv_step(1, lambda zz: y_recv.at[0, zz], ((0, 1), y_send.at[2], y_up))
    kv_step(2, lambda zz: y_recv.at[1, zz], ((2, 3), y_send.at[2], y_down))

    for slot, index, onward, device in ((1, 0, 0, x_up), (2, 1, 1, x_down)):
        for k in (0, 1):
            block = dm_block(slot, k)
            arrive(block, x_recv.at[index, k], x_send.at[0, 0])
            if k == onward:
                send(block, block, x_send.at[2, k], x_recv.at[2, k], device)
            send(block, block, xs_send.at[slot, k], xs_recv.at[x_of[slot], k], sibling)

    kv_step(3, lambda zz: y_recv.at[2, zz], ((), None, None))
    for k in (0, 1):
        block = dm_block(3, k)
        arrive(block, x_recv.at[2, k], x_send.at[0, 0])
        send(block, block, xs_send.at[3, k], xs_recv.at[x_of[3], k], sibling)

    grad_acc[...] = jnp.zeros_like(grad_acc)

    def add_product(from_core):
        def step(i, carry):
            xx, k = i // 2, i % 2
            at = pl.multiple_of((xx * 4 + k * 2 + from_core) * 256, 256)
            grad_acc[...] += lax.dot_general(
                dm_all[from_core, xx, k],
                w_ref[:, pl.ds(at, 256)],
                (((1,), (1,)), ((), ())),
                preferred_element_type=F32,
            )
            return carry

        lax.fori_loop(0, 8, step, 0)

    add_product(core)
    for xx in range(4):
        for k in (0, 1):
            arrive(dm_all.at[1 - core, xx, k], xs_recv.at[xx, k], xs_send.at[0, 0])
    add_product(1 - core)
    grad[...] = grad_acc[...].astype(BF16)

    def grad_args():
        for j in (0, 1):
            for r in (0, 1):
                yield (
                    grad.at[pl.ds(r * 256, 256), pl.ds(j * 128, 128)],
                    da_ref.at[z],
                    g_send.at[j, r],
                    g_recv.at[z],
                    j,
                    r,
                )

    for args in grad_args():
        to_line(*args)

    for slot in range(4):
        for zz in range(4):
            piece = kv_ref.at[y_of[slot], 1 - core, zz]
            arrive(piece, ys_recv.at[slot, zz], ys_send.at[0, zz])
    for zz in range(4):
        arrive(qm_ref.at[zz], a_recv.at[2, zz], a_send.at[2, 0, 0])
    for step in (1, 2, 3):
        arrive(rbm_ref.at[(z - step + 4) % 4], b_recv.at[step - 1], b_send.at[step - 1])
    for zz in range(4):
        arrive(da_ref.at[zz], g_recv.at[zz], g_send.at[0, 0])
    for args in line_args():
        line_sent(*args)
    for args in grad_args():
        line_sent(*args)
    for copy in sent:
        copy.wait_send()


def gather(q, k, v, dm, w, rb):
    vmem = pl.BlockSpec(memory_space=pltpu.VMEM)
    dma = pltpu.SemaphoreType.DMA
    return pl.pallas_call(
        gather_kernel,
        out_shape=(
            jax.ShapeDtypeStruct((4, 2, 4, 2, 256, 128), BF16),
            jax.ShapeDtypeStruct((4, 256, 128), BF16),
            jax.ShapeDtypeStruct((4, 256, 128), BF16),
            jax.ShapeDtypeStruct((4, 8, 128), jnp.int32),
        ),
        in_specs=[vmem] * 6,
        out_specs=(vmem,) * 4,
        scratch_shapes=[
            pltpu.VMEM((2, 4, 2, 512, 256), BF16),
            pltpu.VMEM((512, 256), BF16),
            pltpu.VMEM((512, 256), F32),
            dma((3, 2, 2)),
            dma((3, 4)),
            dma((3,)),
            dma((3,)),
            dma((3, 4)),
            dma((3, 4)),
            dma((4, 4)),
            dma((4, 4)),
            dma((1,)),
            dma((1,)),
            dma((3, 2)),
            dma((3, 2)),
            dma((4, 2)),
            dma((4, 2)),
            dma((2, 2)),
            dma((4,)),
        ],
        compiler_params=pltpu.CompilerParams(
            collective_id=0, has_side_effects=True, vmem_limit_bytes=VMEM_LIMIT
        ),
        name="gather_heads",
    )(q, k, v, dm, w, rb)


def attention_kernel(
    rb_ref, gb_ref, kv_ref, q_ref, da_ref, o_ref, dq_ref, dkv_ref, acc, kcat, vcat
):
    _, y, _, _, core = place()
    scale = HEAD_DIM ** (-0.5)

    def clear(i, carry):
        acc[i] = jnp.zeros((BLOCK, HEAD_DIM), F32)
        return carry

    lax.fori_loop(0, 128, clear, 0, unroll=4)

    def one(n, carry):
        zz, low = n // 2, n % 2
        i = 2 * core + low
        own = (zz * 4 + y) * 4 + i
        ids = [own - 1, own, own + 1]
        ids += [rb_ref[zz, i, t] for t in range(3)]
        ids += [gb_ref[t] for t in range(2)]
        places, biases = [], []
        for t, block in enumerate(ids):
            dead = jnp.logical_or(block < 0, block > 63)
            for earlier in ids[:t]:
                dead = jnp.logical_or(dead, block == earlier)
            block = jnp.clip(block, 0, 63)
            bz, by, bi = block // 16, (block // 4) % 4, block % 4
            places.append(((by * 2 + bi // 2) * 4 + bz) * 4 + bi % 2)
            biases.append(jnp.where(dead, MASKED, 0.0).astype(F32))
        for t, at in enumerate(places):
            kcat[t * BLOCK : (t + 1) * BLOCK, :] = kv_ref[at]
            vcat[t * BLOCK : (t + 1) * BLOCK, :] = kv_ref[at + 2]
        query, grad = q_ref[n], da_ref[n]
        keys, values = kcat[...], vcat[...]
        bias = jnp.concatenate(
            [jnp.full((1, BLOCK), value, F32) for value in biases], axis=1
        )
        contract_last = (((1,), (1,)), ((), ()))
        contract_first = (((0,), (0,)), ((), ()))
        scores = (
            lax.dot_general(query, keys, contract_last, preferred_element_type=F32) * scale
            + bias
        )
        top = jnp.max(scores, axis=1, keepdims=True)
        powers = jnp.exp(scores - top)
        probs = powers * (1.0 / jnp.sum(powers, axis=1, keepdims=True))
        half = probs.astype(BF16)
        out = jnp.dot(half, values, preferred_element_type=F32).astype(BF16)
        o_ref[n] = out
        delta = jnp.sum(out.astype(F32) * grad.astype(F32), axis=1, keepdims=True)
        prob_grad = lax.dot_general(grad, values, contract_last, preferred_element_type=F32)
        score_grad = (probs * (prob_grad - delta) * scale).astype(BF16)
        dq_ref[n] = jnp.dot(score_grad, keys, preferred_element_type=F32).astype(BF16)
        key_add = lax.dot_general(
            score_grad, query, contract_first, preferred_element_type=F32
        )
        value_add = lax.dot_general(half, grad, contract_first, preferred_element_type=F32)
        for t, at in enumerate(places):
            acc[at] += key_add[t * BLOCK : (t + 1) * BLOCK, :]
            acc[at + 2] += value_add[t * BLOCK : (t + 1) * BLOCK, :]
        return carry

    lax.fori_loop(0, 8, one, 0)

    def finish(i, carry):
        dkv_ref[i] = acc[i].astype(BF16)
        return carry

    lax.fori_loop(0, 128, finish, 0, unroll=4)


def attention(rb, gb, kv, q, da):
    vmem = pl.BlockSpec(memory_space=pltpu.VMEM)
    smem = pl.BlockSpec(memory_space=pltpu.SMEM)
    return pl.pallas_call(
        attention_kernel,
        out_shape=(
            jax.ShapeDtypeStruct((8, BLOCK, HEAD_DIM), BF16),
            jax.ShapeDtypeStruct((8, BLOCK, HEAD_DIM), BF16),
            jax.ShapeDtypeStruct((128, BLOCK, HEAD_DIM), BF16),
        ),
        in_specs=[smem, smem, vmem, vmem, vmem],
        out_specs=(vmem,) * 3,
        scratch_shapes=[
            pltpu.VMEM((128, BLOCK, HEAD_DIM), F32),
            pltpu.VMEM((SLOTS * BLOCK, HEAD_DIM), BF16),
            pltpu.VMEM((SLOTS * BLOCK, HEAD_DIM), BF16),
        ],
        compiler_params=pltpu.CompilerParams(vmem_limit_bytes=VMEM_LIMIT),
        name="block_attention",
    )(rb, gb, kv, q, da)


def scatter_kernel(
    o_ref,
    dq_ref,
    p_ref,
    w_ref,
    mixed_ref,
    dqo_ref,
    dko_ref,
    dvo_ref,
    lands,
    attn,
    terms,
    terms_in,
    xa,
    xb,
    xc,
    xd,
    total,
    zb,
    parts,
    parts_in,
    ya,
    yb,
    yc,
    yd,
    final,
    l_send,
    l_recv,
    ps_send,
    ps_recv,
    y_send,
    y_recv,
    xs_send,
    xs_recv,
    x_send,
    x_recv,
    z_send,
    z_recv,
):
    z, y, x, zh, core = place()
    sibling = dev(z, y, x, zh, 1 - core)
    sent = []
    greet()

    def send(src, dst, send_sem, recv_sem, device):
        copy = copy_to(src, dst, send_sem, recv_sem, device)
        copy.start()
        sent.append(copy)

    def arrive(dst, recv_sem, send_sem):
        copy_to(dst, dst, send_sem, recv_sem, sibling).wait_recv()

    y_up, y_down = dev(z, (y + 1) % 4, x, zh, core), dev(z, (y + 3) % 4, x, zh, core)
    x_up, x_down = dev(z, y, (x + 1) % 4, zh, core), dev(z, y, (x + 3) % 4, zh, core)
    far_y, up_y, down_y = (y + 2) % 4, (y + 1) % 4, (y + 3) % 4
    far_x, up_x, down_x = (x + 2) % 4, (x + 1) % 4, (x + 3) % 4

    def back(t, zz, src):
        dst = lands.at[t, z % 2, core]
        return src, dst, l_send.at[t, zz], l_recv.at[t, z % 2, core], zz

    def start_back(src, dst, send_sem, recv_sem, zz):
        here = jnp.logical_and(z == zz, z // 2 == core)

        @pl.when(here)
        def _():
            pltpu.make_async_copy(src, dst, recv_sem).start()

        @pl.when(jnp.logical_not(here))
        def _():
            copy_to(src, dst, send_sem, recv_sem, dev(zz, y, x, zh, z // 2)).start()

    def sent_back(src, dst, send_sem, recv_sem, zz):
        here = jnp.logical_and(z == zz, z // 2 == core)

        @pl.when(jnp.logical_not(here))
        def _():
            copy_to(src, dst, send_sem, recv_sem, dev(zz, y, x, zh, z // 2)).wait_send()

    def landed(t):
        for j in (0, 1):
            for r in (0, 1):
                arrive(lands.at[t, j, r], l_recv.at[t, j, r], l_send.at[t, 0])

    def copy_out(t, out_ref):
        for j in (0, 1):
            for r in (0, 1):
                out_ref[r * 256 : (r + 1) * 256, j * 128 : (j + 1) * 128] = lands[t, j, r]

    for zz in range(4):
        start_back(*back(0, zz, o_ref.at[zz]))
    y_order = (far_y, up_y, down_y, y)
    for n, yy in enumerate(y_order):
        send(p_ref.at[yy, 1 - core], parts_in.at[n], ps_send.at[n], ps_recv.at[n], sibling)
    for zz in range(4):
        start_back(*back(1, zz, dq_ref.at[zz]))

    landed(0)
    copy_out(0, attn)

    def term(to_core, xx):
        for k in (0, 1):
            at = pl.multiple_of((xx * 4 + k * 2 + to_core) * 256, 256)
            terms[to_core, xx, k] = jnp.dot(
                attn[...], w_ref[:, pl.ds(at, 256)], preferred_element_type=F32
            ).astype(BF16)

    x_order = (far_x, up_x, down_x, x)
    for n, xx in enumerate(x_order):
        term(1 - core, xx)
        send(
            terms.at[1 - core, xx], terms_in.at[n], xs_send.at[n], xs_recv.at[n], sibling
        )

    def add_parts(n, yy):
        arrive(parts_in.at[n], ps_recv.at[n], ps_send.at[n])

        def step(i, carry):
            zz, t = i // 2, i % 2
            parts[yy, zz, t] = (
                p_ref[yy, core, zz, t].astype(F32) + parts_in[n, zz, t].astype(F32)
            ).astype(BF16)
            return carry

        lax.fori_loop(0, 8, step, 0)

    add_parts(0, far_y)
    send(parts.at[far_y, pl.ds(0, 2)], ya, y_send.at[0], y_recv.at[0], y_up)
    send(parts.at[far_y, pl.ds(2, 2)], yb, y_send.at[1], y_recv.at[1], y_down)

    def add_terms(n, xx):
        term(core, xx)
        arrive(terms_in.at[n], xs_recv.at[n], xs_send.at[n])
        for k in (0, 1):
            terms[core, xx, k] = (
                terms[core, xx, k].astype(F32) + terms_in[n, k].astype(F32)
            ).astype(BF16)

    add_terms(0, far_x)
    send(terms.at[core, far_x, 0], xa, x_send.at[0], x_recv.at[0], x_up)
    send(terms.at[core, far_x, 1], xb, x_send.at[1], x_recv.at[1], x_down)
    add_parts(1, up_y)
    add_parts(2, down_y)
    add_terms(1, up_x)
    add_terms(2, down_x)

    arrive(ya, y_recv.at[0], y_send.at[0])
    for zz in (0, 1):
        parts[up_y, zz] = (parts[up_y, zz].astype(F32) + ya[zz].astype(F32)).astype(BF16)
    send(parts.at[up_y], yc, y_send.at[2], y_recv.at[2], y_up)
    arrive(yb, y_recv.at[1], y_send.at[1])
    for zz in (0, 1):
        parts[down_y, zz + 2] = (
            parts[down_y, zz + 2].astype(F32) + yb[zz].astype(F32)
        ).astype(BF16)
    send(parts.at[down_y], yd, y_send.at[3], y_recv.at[3], y_down)

    arrive(xa, x_recv.at[0], x_send.at[0])
    terms[core, up_x, 0] = (terms[core, up_x, 0].astype(F32) + xa[...].astype(F32)).astype(BF16)
    send(terms.at[core, up_x], xc, x_send.at[2], x_recv.at[2], x_up)
    arrive(xb, x_recv.at[1], x_send.at[1])
    terms[core, down_x, 1] = (
        terms[core, down_x, 1].astype(F32) + xb[...].astype(F32)
    ).astype(BF16)
    send(terms.at[core, down_x], xd, x_send.at[3], x_recv.at[3], x_down)

    add_terms(3, x)
    arrive(parts_in.at[3], ps_recv.at[3], ps_send.at[3])
    landed(1)
    copy_out(1, dqo_ref)

    arrive(xc, x_recv.at[2], x_send.at[2])
    arrive(xd, x_recv.at[3], x_send.at[3])

    def add_total(k):
        total[k] = (
            terms[core, x, k].astype(F32) + xc[k].astype(F32) + xd[k].astype(F32)
        ).astype(BF16)

    add_total(1 - zh)
    send(total.at[1 - zh], zb, z_send.at[0], z_recv.at[0], dev(z, y, x, 1 - zh, core))
    add_total(zh)

    arrive(yc, y_recv.at[2], y_send.at[2])
    arrive(yd, y_recv.at[3], y_send.at[3])

    def add_final(i, carry):
        zz, t = i // 2, i % 2
        final[zz, t] = (
            p_ref[y, core, zz, t].astype(F32)
            + parts_in[3, zz, t].astype(F32)
            + yc[zz, t].astype(F32)
            + yd[zz, t].astype(F32)
        ).astype(BF16)
        return carry

    lax.fori_loop(0, 8, add_final, 0)
    for zz in range(4):
        for t in (0, 1):
            start_back(*back(2 + t, zz, final.at[zz, t]))

    arrive(zb, z_recv.at[0], z_send.at[0])
    mixed_ref[...] = (total[zh].astype(F32) + zb[...].astype(F32)).astype(BF16)
    landed(2)
    copy_out(2, dko_ref)
    landed(3)
    copy_out(3, dvo_ref)
    for zz in range(4):
        sent_back(*back(0, zz, o_ref.at[zz]))
        sent_back(*back(1, zz, dq_ref.at[zz]))
        for t in (0, 1):
            sent_back(*back(2 + t, zz, final.at[zz, t]))
    for copy in sent:
        copy.wait_send()


def scatter(o, dq, dkv, w):
    vmem = pl.BlockSpec(memory_space=pltpu.VMEM)
    dma = pltpu.SemaphoreType.DMA
    return pl.pallas_call(
        scatter_kernel,
        out_shape=(jax.ShapeDtypeStruct((512, 256), BF16),) * 4,
        in_specs=[vmem] * 4,
        out_specs=(vmem,) * 4,
        scratch_shapes=[
            pltpu.VMEM((4, 2, 2, 256, 128), BF16),
            pltpu.VMEM((512, 256), BF16),
            pltpu.VMEM((2, 4, 2, 512, 256), BF16),
            pltpu.VMEM((4, 2, 512, 256), BF16),
            pltpu.VMEM((512, 256), BF16),
            pltpu.VMEM((512, 256), BF16),
            pltpu.VMEM((2, 512, 256), BF16),
            pltpu.VMEM((2, 512, 256), BF16),
            pltpu.VMEM((2, 512, 256), BF16),
            pltpu.VMEM((512, 256), BF16),
            pltpu.VMEM((4, 4, 2, 256, 128), BF16),
            pltpu.VMEM((4, 4, 2, 256, 128), BF16),
            pltpu.VMEM((2, 2, 256, 128), BF16),
            pltpu.VMEM((2, 2, 256, 128), BF16),
            pltpu.VMEM((4, 2, 256, 128), BF16),
            pltpu.VMEM((4, 2, 256, 128), BF16),
            pltpu.VMEM((4, 2, 256, 128), BF16),
            dma((4, 4)),
            dma((4, 2, 2)),
            dma((4,)),
            dma((4,)),
            dma((4,)),
            dma((4,)),
            dma((4,)),
            dma((4,)),
            dma((4,)),
            dma((4,)),
            dma((1,)),
            dma((1,)),
        ],
        compiler_params=pltpu.CompilerParams(
            collective_id=1, has_side_effects=True, vmem_limit_bytes=VMEM_LIMIT
        ),
        name="scatter_heads",
    )(o, dq, dkv, w)


def body(queries, keys, values, w_out, d_mixed, random_blocks, global_blocks):
    rb = jnp.pad(random_blocks, ((0, 4), (0, 125)))
    kv, q, da, rb = gather(queries, keys, values, d_mixed, w_out, rb)
    o, dq, dkv = attention(
        rb,
        global_blocks,
        kv.reshape(128, BLOCK, HEAD_DIM),
        q.reshape(8, BLOCK, HEAD_DIM),
        da.reshape(8, BLOCK, HEAD_DIM),
    )
    return scatter(
        o.reshape(4, 256, 128),
        dq.reshape(4, 256, 128),
        dkv.reshape(4, 2, 4, 2, 256, 128),
        w_out,
    )


def solution(mesh):
    return jax.shard_map(
        body,
        mesh=mesh,
        in_specs=(
            P("seq", "head"),
            P("seq", "head"),
            P("seq", "head"),
            P("head", None),
            P("seq", "head"),
            P("seq", None),
            P(),
        ),
        out_specs=(P("seq", "head"), P("seq", "head"), P("seq", "head"), P("seq", "head")),
        check_vma=False,
    )
```

time: 1490 us -> 153 us (0.10)
  the two profiles are of different devices: /device:TPU:82 before, /device:TPU:1 now
where the time goes in v1:
time: 153 us; the launch traced here: 151 us
  Pallas kernels  143 us (93%)
  local copies, waits for them, and re-layouts  7.95 us (5%)
    pallas_call x1, Pallas kernels, gather(): pl.pallas_call(gather_kernel, out_shape=(jax.ShapeDtypeStruct((4, 2, 4, 2...  69.3 us
    pallas_call x1, Pallas kernels, scatter(): pl.pallas_call(scatter_kernel, out_shape=(jax.ShapeDtypeStruct((512, 256)...  58.6 us
    pallas_call x1, Pallas kernels, attention(): pl.pallas_call(attention_kernel, out_shape=(jax.ShapeDtypeStruct((8, BLOC...  14.8 us
    unnamed x4, local copies, waits for them, and re-layouts  6.68 us

profile of v1, /device:TPU:1, one launch (start us, length us, event | category | flops | bytes accessed | tf_op | source)
XLA Modules:
  0.0 151.2 jit_solution(1274751628720036997)
XLA Ops:
  0.6 1.3 pad.4.rb_ref
  1.9 69.3 %gather_heads.1 = (bf16[4,2,4,2,256,128]{5,4,3,2,1,0:T(8,128)(2,1)}, bf16[4,256,128]{2,1,0:T(8,128)(2,1)}, bf16[4,256,128]{2,1,0:T(8,128)(2,1)}, s32[4,8,128]{2,1,0:T(8,128)}) custom-call(bf16[512,256]{1,0:T(8,128)(2,1)} %q_ref.1, bf16[512,256]{1,0:T(8,128)(2,1)} %k_ref.1, bf16[512,256]{1,0:T(8,128)(2,1)} %v_ref.1, bf16[512,256]{1,0:T(8,128)(2,1)} %dm_ref.1, ...), custom_call_target="tpu_custom_call" | custom-call | tf_op jit(solution)/shard_map/gather_heads/pallas_call | solution.py:267
  71.2 14.8 %block_attention.1 = (bf16[8,128,128]{2,1,0:T(8,128)(2,1)}, bf16[8,128,128]{2,1,0:T(8,128)(2,1)}, bf16[128,128,128]{2,1,0:T(8,128)(2,1)}) custom-call(s32[4,8,128]{2,1,0:T(8,128)} %get-tuple-element.11.rb_ref, s32[2]{0:T(128)} %gb_ref.1, bf16[128,128,128]{2,1,0:T(8,128)(2,1)} %bitcast.6, bf16[8,128,128]{2,1,0:T(8,128)(2,1)} %bitcast.8, ...), custom_call_target="tpu_custom_call" | custom-call | tf_op jit(solution)/shard_map/block_attention/pallas_call | solution.py:378
  85.9 58.6 %scatter_heads.1 = (bf16[512,256]{1,0:T(8,128)(2,1)}, bf16[512,256]{1,0:T(8,128)(2,1)}, bf16[512,256]{1,0:T(8,128)(2,1)}, bf16[512,256]{1,0:T(8,128)(2,1)}) custom-call(bf16[4,256,128]{2,1,0:T(8,128)(2,1)} %bitcast.10, bf16[4,256,128]{2,1,0:T(8,128)(2,1)} %bitcast.11, bf16[4,2,4,2,256,128]{5,4,3,2,1,0:T(8,128)(2,1)} %bitcast.7, bf16[256,4096]{1,0:T(8,128)(2,1)} %w_ref.3), custom_call_target="tpu_custom_call" | custom-call | tf_op jit(solution)/shard_map/scatter_heads/pallas_call | solution.py:616
  144.5 1.7 %copy.15 = bf16[512,256]{1,0:T(8,128)(2,1)} copy(bf16[512,256]{1,0:T(8,128)(2,1)} %get-tuple-element.22) | data formatting | bytes 524288
  146.2 1.7 %copy.16 = bf16[512,256]{1,0:T(8,128)(2,1)} copy(bf16[512,256]{1,0:T(8,128)(2,1)} %get-tuple-element.23) | data formatting | bytes 524288
  147.9 1.7 %copy.17 = bf16[512,256]{1,0:T(8,128)(2,1)} copy(bf16[512,256]{1,0:T(8,128)(2,1)} %get-tuple-element.24) | data formatting | bytes 524288
  149.5 1.7 %copy.18 = bf16[512,256]{1,0:T(8,128)(2,1)} copy(bf16[512,256]{1,0:T(8,128)(2,1)} %get-tuple-element.25) | data formatting | bytes 524288

commit v2 on v1

v2 whole, which is shorter than its diff:
```python
import jax
import jax.numpy as jnp
from jax import lax
from jax.experimental import pallas as pl
from jax.experimental.pallas import tpu as pltpu
from jax.sharding import PartitionSpec as P

HEAD_DIM = 128
BLOCK = 128
SLOTS = 8
MASKED = -1e30
CONTRACT_LAST = (((1,), (1,)), ((), ()))
CONTRACT_FIRST = (((0,), (0,)), ((), ()))
MESH = pl.DeviceIdType.MESH
BF16 = jnp.bfloat16
F32 = jnp.float32
VMEM_LIMIT = 56 * 1024 * 1024


def place():
    seq, head = lax.axis_index("seq"), lax.axis_index("head")
    return seq // 4, seq % 4, head // 4, (head // 2) % 2, head % 2


def dev(z, y, x, zh, core):
    return (z * 4 + y, x * 4 + zh * 2 + core)


def copy_to(src, dst, send_sem, recv_sem, device):
    return pltpu.make_async_remote_copy(
        src_ref=src,
        dst_ref=dst,
        send_sem=send_sem,
        recv_sem=recv_sem,
        device_id=device,
        device_id_type=MESH,
    )


def greet():
    z, y, x, zh, core = place()
    barrier = pltpu.get_barrier_semaphore()
    others = [dev(z, y, x, zh, 1 - core)]
    for step in (1, 2, 3):
        for r in (0, 1):
            others.append(dev((z + step) % 4, y, x, zh, r))
    others += [dev(z, (y + 1) % 4, x, zh, core), dev(z, (y + 3) % 4, x, zh, core)]
    others += [dev(z, y, (x + 1) % 4, zh, core), dev(z, y, (x + 3) % 4, zh, core)]
    others.append(dev(z, y, x, 1 - zh, core))
    for other in others:
        pl.semaphore_signal(barrier, inc=1, device_id=other, device_id_type=MESH)
    pl.semaphore_wait(barrier, len(others))


def slot_table(random_ref, global_ref):
    first = lax.axis_index("seq") * 4
    rows = lax.broadcasted_iota(jnp.int32, (8, 128), 0)
    lanes = lax.broadcasted_iota(jnp.int32, (8, 128), 1)
    table = jnp.zeros((8, 128), jnp.int32)
    for i in range(4):
        own = first + i
        ids = [own - 1, own, own + 1]
        ids += [random_ref[i, t] for t in range(3)]
        ids += [global_ref[t] for t in range(2)]
        for t, block in enumerate(ids):
            dead = jnp.logical_or(block < 0, block > 63)
            for earlier in ids[:t]:
                dead = jnp.logical_or(dead, block == earlier)
            block = jnp.minimum(jnp.maximum(block, 0), 63)
            at = ((block >> 2) & 3) * 32 + ((block >> 1) & 1) * 16 + (block >> 4) * 2 + (block & 1)
            here = rows == i
            table = jnp.where(jnp.logical_and(here, lanes == t), at, table)
            table = jnp.where(
                jnp.logical_and(here, lanes == SLOTS + t), dead.astype(jnp.int32), table
            )
    return table


def gather_kernel(
    q_ref,
    k_ref,
    v_ref,
    dm_ref,
    w_ref,
    random_ref,
    global_ref,
    tables_ref,
    qm_ref,
    da_ref,
    probs_ref,
    scores_ref,
    dq_ref,
    ol_ref,
    kv_ref,
    table_ref,
    dm_all,
    grad,
    grad_acc,
    ids_ref,
    outs,
    full,
    kcat,
    vcat,
    id_sem,
    a_send,
    a_recv,
    b_send,
    b_recv,
    y_send,
    y_recv,
    ys_send,
    ys_recv,
    z_send,
    z_recv,
    x_send,
    x_recv,
    xs_send,
    xs_recv,
    g_send,
    g_recv,
    o_send,
    o_recv,
):
    z, y, x, zh, core = place()
    sibling = dev(z, y, x, zh, 1 - core)
    sent = []
    table_ref[...] = slot_table(random_ref, global_ref)
    greet()

    def send(src, dst, send_sem, recv_sem, device):
        copy = copy_to(src, dst, send_sem, recv_sem, device)
        copy.start()
        sent.append(copy)

    def arrive(dst, recv_sem, send_sem):
        copy_to(dst, dst, send_sem, recv_sem, sibling).wait_recv()

    y_up, y_down = dev(z, (y + 1) % 4, x, zh, core), dev(z, (y + 3) % 4, x, zh, core)
    x_up, x_down = dev(z, y, (x + 1) % 4, zh, core), dev(z, y, (x + 3) % 4, zh, core)
    partner = dev(z, y, x, 1 - zh, core)
    y_of = (y, (y + 3) % 4, (y + 1) % 4, (y + 2) % 4)
    x_of = (x, (x + 3) % 4, (x + 1) % 4, (x + 2) % 4)

    def to_line(src, dst, send_sem, recv_sem, j, r):
        there = 2 * core + j
        here = jnp.logical_and(there == z, core == r)

        @pl.when(here)
        def _():
            pltpu.make_async_copy(src, dst, recv_sem).start()

        @pl.when(jnp.logical_not(here))
        def _():
            copy_to(src, dst, send_sem, recv_sem, dev(there, y, x, zh, r)).start()

    def line_sent(src, dst, send_sem, recv_sem, j, r):
        there = 2 * core + j
        here = jnp.logical_and(there == z, core == r)

        @pl.when(jnp.logical_not(here))
        def _():
            copy_to(src, dst, send_sem, recv_sem, dev(there, y, x, zh, r)).wait_send()

    def piece(src, j, r):
        return src.at[pl.ds(2 * r, 2), :, pl.ds(j * 128, 128)]

    def kv_at(yy, r, t, zz, count):
        return kv_ref.at[pl.ds((((yy * 2 + r) * 2 + t) * 4 + zz) * 2, 2 * count)]

    def kv_args(t):
        for j in (0, 1):
            for r in (0, 1):
                yield (
                    piece((k_ref, v_ref)[t], j, r),
                    kv_at(y, r, t, z, 1),
                    a_send.at[t, j, r],
                    a_recv.at[t, z],
                    j,
                    r,
                )

    def query_args():
        for j in (0, 1):
            for r in (0, 1):
                yield (
                    piece(q_ref, j, r),
                    qm_ref.at[pl.ds(2 * z, 2)],
                    a_send.at[2, j, r],
                    a_recv.at[2, z],
                    j,
                    r,
                )

    def grad_args(r):
        for j in (0, 1):
            yield (
                piece(grad, j, r),
                da_ref.at[pl.ds(2 * z, 2)],
                g_send.at[j, r],
                g_recv.at[z],
                j,
                r,
            )

    def dm_block(wave, slot, late):
        return dm_all.at[wave, core, x_of[slot], (1 - zh) if late else zh]

    def own_rows(wave):
        return dm_ref.at[pl.ds(wave * 256, 256)]

    def dm_to_sibling(wave, slot, late, src):
        k = (1 - zh) if late else zh
        send(
            src,
            dm_block(wave, slot, late),
            xs_send.at[wave, slot, late],
            xs_recv.at[wave, x_of[slot], k],
            sibling,
        )

    def dm_to_ring(wave, late, src):
        dst = dm_block(wave, 0, late)
        send(src, dst, x_send.at[wave, late, 0], x_recv.at[wave, late, 0], x_up)
        send(src, dst, x_send.at[wave, late, 1], x_recv.at[wave, late, 1], x_down)
        dm_to_sibling(wave, 0, late, src)

    def dm_to_partner(wave):
        send(
            own_rows(wave),
            dm_block(wave, 0, 0),
            z_send.at[wave],
            z_recv.at[wave],
            partner,
        )

    def dm_from_partner(wave):
        block = dm_block(wave, 0, 1)
        arrive(block, z_recv.at[wave], z_send.at[wave])
        dm_to_ring(wave, 1, block)

    def dm_from_ring(wave, late):
        for side in (0, 1):
            block = dm_block(wave, 1 + side, late)
            arrive(block, x_recv.at[wave, late, side], x_send.at[wave, late, side])
            if side == (wave + late) % 2:
                send(
                    block,
                    block,
                    x_send.at[wave, late, 2],
                    x_recv.at[wave, late, 2],
                    (x_up, x_down)[side],
                )
            dm_to_sibling(wave, 1 + side, late, block)

    def dm_from_far(wave, late):
        block = dm_block(wave, 3, late)
        arrive(block, x_recv.at[wave, late, 2], x_send.at[wave, late, 2])
        dm_to_sibling(wave, 3, late, block)

    def kv_from_line(t):
        for zz in range(4):
            arrive(kv_at(y, core, t, zz, 1), a_recv.at[t, zz], a_send.at[t, 0, 0])
        own = kv_at(y, core, t, 0, 4)
        send(own, own, y_send.at[t, 0], y_recv.at[t, 0], y_up)
        send(own, own, y_send.at[t, 1], y_recv.at[t, 1], y_down)
        send(own, own, ys_send.at[t, 0], ys_recv.at[t, 0], sibling)

    def kv_from_ring(t):
        for side in (0, 1):
            block = kv_at(y_of[1 + side], core, t, 0, 4)
            arrive(block, y_recv.at[t, side], y_send.at[t, side])
            part = kv_at(y_of[1 + side], core, t, 2 * side, 2)
            send(
                part,
                part,
                y_send.at[t, 2 + side],
                y_recv.at[t, 2 + side],
                (y_up, y_down)[side],
            )
            send(block, block, ys_send.at[t, 1 + side], ys_recv.at[t, 1 + side], sibling)

    def kv_from_far(t):
        for side in (0, 1):
            part = kv_at(y_of[3], core, t, 2 * side, 2)
            arrive(part, y_recv.at[t, 2 + side], y_send.at[t, 2 + side])
        block = kv_at(y_of[3], core, t, 0, 4)
        send(block, block, ys_send.at[t, 3], ys_recv.at[t, 3], sibling)

    def add_product(wave, from_core, fresh):
        if fresh:
            grad_acc[...] = jnp.zeros_like(grad_acc)

        def step(i, carry):
            xx, k = i // 2, i % 2
            at = pl.multiple_of((xx * 4 + k * 2 + from_core) * 256, 256)
            grad_acc[...] += lax.dot_general(
                dm_all[wave, from_core, xx, k],
                w_ref[:, pl.ds(at, 256)],
                CONTRACT_LAST,
                preferred_element_type=F32,
            )
            return carry

        lax.fori_loop(0, 8, step, 0)

    def make_grad(wave):
        add_product(wave, core, True)
        for xx in range(4):
            for k in (0, 1):
                arrive(
                    dm_all.at[wave, 1 - core, xx, k],
                    xs_recv.at[wave, xx, k],
                    xs_send.at[wave, 0, 0],
                )
        add_product(wave, 1 - core, False)
        grad[2 * wave] = grad_acc[:128, :].astype(BF16)
        grad[2 * wave + 1] = grad_acc[128:, :].astype(BF16)
        for args in grad_args(wave):
            to_line(*args)

    for args in kv_args(0):
        to_line(*args)
    dm_to_partner(0)
    for wave in (0, 1):
        dm_to_ring(wave, 0, own_rows(wave))
    for args in kv_args(1):
        to_line(*args)
    dm_to_partner(1)
    for step in (1, 2, 3):
        send(
            table_ref,
            tables_ref.at[z],
            b_send.at[step - 1],
            b_recv.at[step - 1],
            dev((z + step) % 4, y, x, zh, core),
        )
    tables_ref[z] = table_ref[...]
    for wave in (0, 1):
        dm_all[wave, core, x, zh] = dm_ref[wave * 256 : (wave + 1) * 256, :]

    kv_from_line(0)
    dm_from_partner(0)
    dm_from_ring(0, 0)
    dm_from_ring(1, 0)
    kv_from_line(1)
    for args in query_args():
        to_line(*args)
    dm_from_partner(1)
    kv_from_ring(0)
    dm_from_ring(0, 1)
    kv_from_ring(1)
    dm_from_far(0, 0)
    dm_from_far(1, 0)
    dm_from_far(0, 1)
    dm_from_ring(1, 1)
    kv_from_far(0)
    make_grad(0)
    dm_from_far(1, 1)
    kv_from_far(1)
    make_grad(1)

    for step in (1, 2, 3):
        arrive(tables_ref.at[(z - step + 4) % 4], b_recv.at[step - 1], b_send.at[step - 1])
    to_smem = pltpu.make_async_copy(tables_ref, ids_ref, id_sem.at[0])
    to_smem.start()
    for t in (0, 1):
        for slot in range(4):
            arrive(kv_at(y_of[slot], 1 - core, t, 0, 4), ys_recv.at[t, slot], ys_send.at[t, 0])
    for zz in range(4):
        arrive(qm_ref.at[pl.ds(2 * zz, 2)], a_recv.at[2, zz], a_send.at[2, 0, 0])
    to_smem.wait()

    scale = HEAD_DIM ** (-0.5)

    def forward(n, carry):
        zz, i = n // 2, 2 * core + n % 2
        for t in range(SLOTS):
            at = ids_ref[zz, i, t]
            kcat[n, t * BLOCK : (t + 1) * BLOCK, :] = kv_ref[at]
            vcat[n, t * BLOCK : (t + 1) * BLOCK, :] = kv_ref[at + 8]
        bias = jnp.concatenate(
            [
                jnp.full((1, BLOCK), ids_ref[zz, i, SLOTS + t].astype(F32) * MASKED, F32)
                for t in range(SLOTS)
            ],
            axis=1,
        )
        scores = (
            lax.dot_general(qm_ref[n], kcat[n], CONTRACT_LAST, preferred_element_type=F32)
            * scale
            + bias
        )
        top = jnp.max(scores, axis=1, keepdims=True)
        powers = jnp.exp(scores - top)
        probs = powers * (1.0 / jnp.sum(powers, axis=1, keepdims=True))
        full[n] = probs
        half = probs.astype(BF16)
        probs_ref[n] = half
        outs[n] = jnp.dot(half, vcat[n], preferred_element_type=F32).astype(BF16)
        return carry

    lax.fori_loop(0, 8, forward, 0)

    def out_here(zz):
        return jnp.logical_and(z == zz, z // 2 == core)

    def out_piece(zz):
        return outs.at[pl.ds(2 * zz, 2)]

    def out_copy(zz):
        return copy_to(
            out_piece(zz),
            ol_ref.at[z % 2, core],
            o_send.at[zz],
            o_recv.at[z % 2, core],
            dev(zz, y, x, zh, z // 2),
        )

    for zz in range(4):

        @pl.when(out_here(zz))
        def _():
            pltpu.make_async_copy(
                out_piece(zz), ol_ref.at[z % 2, core], o_recv.at[z % 2, core]
            ).start()

        @pl.when(jnp.logical_not(out_here(zz)))
        def _():
            out_copy(zz).start()

    for zz in range(4):
        arrive(da_ref.at[pl.ds(2 * zz, 2)], g_recv.at[zz], g_send.at[0, 0])

    def backward(n, carry):
        grad_rows = da_ref[n]
        delta = jnp.sum(outs[n].astype(F32) * grad_rows.astype(F32), axis=1, keepdims=True)
        prob_grad = lax.dot_general(
            grad_rows, vcat[n], CONTRACT_LAST, preferred_element_type=F32
        )
        score_grad = (full[n] * (prob_grad - delta) * scale).astype(BF16)
        scores_ref[n] = score_grad
        dq_ref[n] = jnp.dot(score_grad, kcat[n], preferred_element_type=F32).astype(BF16)
        return carry

    lax.fori_loop(0, 8, backward, 0)

    for j in (0, 1):
        for r in (0, 1):
            arrive(ol_ref.at[j, r], o_recv.at[j, r], o_send.at[0])
    for t in (0, 1):
        for args in kv_args(t):
            line_sent(*args)
        for args in grad_args(t):
            line_sent(*args)
    for args in query_args():
        line_sent(*args)
    for zz in range(4):

        @pl.when(jnp.logical_not(out_here(zz)))
        def _():
            out_copy(zz).wait_send()

    for copy in sent:
        copy.wait_send()


def gather(q, k, v, dm, w, random_blocks, global_blocks):
    vmem = pl.BlockSpec(memory_space=pltpu.VMEM)
    smem = pl.BlockSpec(memory_space=pltpu.SMEM)
    dma = pltpu.SemaphoreType.DMA
    blocks = jax.ShapeDtypeStruct((8, BLOCK, HEAD_DIM), BF16)
    weights = jax.ShapeDtypeStruct((8, BLOCK, SLOTS * BLOCK), BF16)
    return pl.pallas_call(
        gather_kernel,
        out_shape=(
            jax.ShapeDtypeStruct((4, 8, 128), jnp.int32),
            blocks,
            blocks,
            weights,
            weights,
            blocks,
            jax.ShapeDtypeStruct((2, 2, 2, BLOCK, HEAD_DIM), BF16),
        ),
        in_specs=[vmem] * 5 + [smem] * 2,
        out_specs=(vmem,) * 7,
        scratch_shapes=[
            pltpu.VMEM((128, BLOCK, HEAD_DIM), BF16),
            pltpu.VMEM((8, 128), jnp.int32),
            pltpu.VMEM((2, 2, 4, 2, 256, 256), BF16),
            pltpu.VMEM((4, BLOCK, 256), BF16),
            pltpu.VMEM((256, 256), F32),
            pltpu.SMEM((4, 8, 128), jnp.int32),
            pltpu.VMEM((8, BLOCK, HEAD_DIM), BF16),
            pltpu.VMEM((8, BLOCK, SLOTS * BLOCK), F32),
            pltpu.VMEM((8, SLOTS * BLOCK, HEAD_DIM), BF16),
            pltpu.VMEM((8, SLOTS * BLOCK, HEAD_DIM), BF16),
            dma((1,)),
            dma((3, 2, 2)),
            dma((3, 4)),
            dma((3,)),
            dma((3,)),
            dma((2, 4)),
            dma((2, 4)),
            dma((2, 4)),
            dma((2, 4)),
            dma((2,)),
            dma((2,)),
            dma((2, 2, 3)),
            dma((2, 2, 3)),
            dma((2, 4, 2)),
            dma((2, 4, 2)),
            dma((2, 2)),
            dma((4,)),
            dma((4,)),
            dma((2, 2)),
        ],
        compiler_params=pltpu.CompilerParams(
            collective_id=0, has_side_effects=True, vmem_limit_bytes=VMEM_LIMIT
        ),
        name="gather_heads",
    )(q, k, v, dm, w, random_blocks, global_blocks)


def key_grads_kernel(ids_ref, q_ref, da_ref, probs_ref, scores_ref, dkv_ref, acc):
    core = place()[4]

    def clear(i, carry):
        acc[i] = jnp.zeros((BLOCK, HEAD_DIM), F32)
        return carry

    lax.fori_loop(0, 128, clear, 0, unroll=8)

    def one(n, carry):
        key_add = lax.dot_general(
            scores_ref[n], q_ref[n], CONTRACT_FIRST, preferred_element_type=F32
        )
        value_add = lax.dot_general(
            probs_ref[n], da_ref[n], CONTRACT_FIRST, preferred_element_type=F32
        )
        for t in range(SLOTS):
            at = ids_ref[n // 2, 2 * core + n % 2, t]
            acc[at] += key_add[t * BLOCK : (t + 1) * BLOCK, :]
            acc[at + 8] += value_add[t * BLOCK : (t + 1) * BLOCK, :]
        return carry

    lax.fori_loop(0, 8, one, 0, unroll=2)

    def finish(i, carry):
        dkv_ref[i] = acc[i].astype(BF16)
        return carry

    lax.fori_loop(0, 128, finish, 0, unroll=8)


def key_grads(ids, q, da, probs, scores):
    vmem = pl.BlockSpec(memory_space=pltpu.VMEM)
    smem = pl.BlockSpec(memory_space=pltpu.SMEM)
    return pl.pallas_call(
        key_grads_kernel,
        out_shape=jax.ShapeDtypeStruct((128, BLOCK, HEAD_DIM), BF16),
        in_specs=[smem, vmem, vmem, vmem, vmem],
        out_specs=vmem,
        scratch_shapes=[pltpu.VMEM((128, BLOCK, HEAD_DIM), F32)],
        compiler_params=pltpu.CompilerParams(vmem_limit_bytes=VMEM_LIMIT),
        name="key_grads",
    )(ids, q, da, probs, scores)


def unpack(pieces, out_ref):
    for j in (0, 1):
        for r in (0, 1):
            for low in (0, 1):
                row = (2 * r + low) * BLOCK
                out_ref[row : row + BLOCK, j * 128 : (j + 1) * 128] = pieces[j, r, low]


def scatter_kernel(
    ol_ref,
    dq_ref,
    p_ref,
    w_ref,
    mixed_ref,
    lands,
    attn,
    terms,
    terms_in,
    xa,
    xc,
    total,
    zb,
    parts,
    parts_in,
    ya,
    yc,
    final,
    l_send,
    l_recv,
    ps_send,
    ps_recv,
    y_send,
    y_recv,
    xs_send,
    xs_recv,
    x_send,
    x_recv,
    z_send,
    z_recv,
):
    z, y, x, zh, core = place()
    sibling = dev(z, y, x, zh, 1 - core)
    sent = []
    greet()

    def send(src, dst, send_sem, recv_sem, device):
        copy = copy_to(src, dst, send_sem, recv_sem, device)
        copy.start()
        sent.append(copy)

    def arrive(dst, recv_sem, send_sem):
        copy_to(dst, dst, send_sem, recv_sem, sibling).wait_recv()

    y_dev = (dev(z, (y + 1) % 4, x, zh, core), dev(z, (y + 3) % 4, x, zh, core))
    x_dev = (dev(z, y, (x + 1) % 4, zh, core), dev(z, y, (x + 3) % 4, zh, core))
    y_of = ((y + 2) % 4, (y + 1) % 4, (y + 3) % 4, y)
    x_of = ((x + 2) % 4, (x + 1) % 4, (x + 3) % 4, x)

    def back(t, zz, src):
        dst = lands.at[t, z % 2, core]
        return src, dst, l_send.at[t, zz], l_recv.at[t, z % 2, core], zz

    def start_back(src, dst, send_sem, recv_sem, zz):
        here = jnp.logical_and(z == zz, z // 2 == core)

        @pl.when(here)
        def _():
            pltpu.make_async_copy(src, dst, recv_sem).start()

        @pl.when(jnp.logical_not(here))
        def _():
            copy_to(src, dst, send_sem, recv_sem, dev(zz, y, x, zh, z // 2)).start()

    def sent_back(src, dst, send_sem, recv_sem, zz):
        here = jnp.logical_and(z == zz, z // 2 == core)

        @pl.when(jnp.logical_not(here))
        def _():
            copy_to(src, dst, send_sem, recv_sem, dev(zz, y, x, zh, z // 2)).wait_send()

    def landed(t):
        for j in (0, 1):
            for r in (0, 1):
                arrive(lands.at[t, j, r], l_recv.at[t, j, r], l_send.at[t, 0])

    def query_piece(zz):
        return dq_ref.at[pl.ds(2 * zz, 2)]

    def parts_to_sibling(t):
        for n in range(4):
            send(
                p_ref.at[y_of[n], 1 - core, t],
                parts_in.at[t, n],
                ps_send.at[t, n],
                ps_recv.at[t, n],
                sibling,
            )

    def add_parts(t, n, zz, more):
        value = p_ref[y_of[n], core, t, zz].astype(F32) + parts_in[t, n, zz].astype(F32)
        for ref in more:
            value += ref.astype(F32)
        return value.astype(BF16)

    def parts_here(t, n):
        arrive(parts_in.at[t, n], ps_recv.at[t, n], ps_send.at[t, n])

    def parts_far(t):
        parts_here(t, 0)
        for side in (0, 1):
            for zz in (2 * side, 2 * side + 1):
                parts[t, 0, zz] = add_parts(t, 0, zz, ())
            send(
                parts.at[t, 0, pl.ds(2 * side, 2)],
                ya.at[t, side],
                y_send.at[t, side],
                y_recv.at[t, side],
                y_dev[side],
            )

    def parts_near(t):
        for side in (0, 1):
            n = 1 + side
            parts_here(t, n)
            for zz in (2 - 2 * side, 3 - 2 * side):
                parts[t, n, zz] = add_parts(t, n, zz, ())
            arrive(ya.at[t, side], y_recv.at[t, side], y_send.at[t, side])
            for low in (0, 1):
                zz = 2 * side + low
                parts[t, n, zz] = add_parts(t, n, zz, (ya[t, side, low],))
            send(
                parts.at[t, n],
                yc.at[t, side],
                y_send.at[t, n + 1],
                y_recv.at[t, n + 1],
                y_dev[side],
            )

    def parts_end(t):
        parts_here(t, 3)
        for side in (0, 1):
            arrive(yc.at[t, side], y_recv.at[t, 2 + side], y_send.at[t, 2 + side])
        for zz in range(4):
            final[t, zz] = add_parts(t, 3, zz, (yc[t, 0, zz], yc[t, 1, zz]))
            start_back(*back(1 + t, zz, final.at[t, zz]))

    def make_terms(wave, to_core, n):
        for k in (0, 1):
            at = pl.multiple_of((x_of[n] * 4 + k * 2 + to_core) * 256, 256)
            terms[wave, to_core, n, k] = jnp.dot(
                attn[wave * 256 : (wave + 1) * 256, :],
                w_ref[:, pl.ds(at, 256)],
                preferred_element_type=F32,
            ).astype(BF16)

    def terms_to_sibling(wave):
        for n in range(4):
            make_terms(wave, 1 - core, n)
            send(
                terms.at[wave, 1 - core, n],
                terms_in.at[wave, n],
                xs_send.at[wave, n],
                xs_recv.at[wave, n],
                sibling,
            )

    def terms_here(wave, n):
        make_terms(wave, core, n)
        arrive(terms_in.at[wave, n], xs_recv.at[wave, n], xs_send.at[wave, n])

    def add_terms(wave, n, k, more):
        value = terms[wave, core, n, k].astype(F32) + terms_in[wave, n, k].astype(F32)
        for ref in more:
            value += ref.astype(F32)
        return value.astype(BF16)

    def terms_far(wave):
        terms_here(wave, 0)
        for k in (0, 1):
            terms[wave, core, 0, k] = add_terms(wave, 0, k, ())
            send(
                terms.at[wave, core, 0, k],
                xa.at[wave, k],
                x_send.at[wave, k],
                x_recv.at[wave, k],
                x_dev[k],
            )

    def terms_near(wave):
        for side in (0, 1):
            n = 1 + side
            terms_here(wave, n)
            arrive(xa.at[wave, side], x_recv.at[wave, side], x_send.at[wave, side])
            terms[wave, core, n, side] = add_terms(wave, n, side, (xa[wave, side],))
            terms[wave, core, n, 1 - side] = add_terms(wave, n, 1 - side, ())
            send(
                terms.at[wave, core, n],
                xc.at[wave, side],
                x_send.at[wave, n + 1],
                x_recv.at[wave, n + 1],
                x_dev[side],
            )

    def terms_end(wave):
        terms_here(wave, 3)
        for side in (0, 1):
            arrive(xc.at[wave, side], x_recv.at[wave, 2 + side], x_send.at[wave, 2 + side])

        def add_total(k):
            total[wave, k] = add_terms(wave, 3, k, (xc[wave, 0, k], xc[wave, 1, k]))

        add_total(1 - zh)
        send(
            total.at[wave, 1 - zh],
            zb.at[wave],
            z_send.at[wave],
            z_recv.at[wave],
            dev(z, y, x, 1 - zh, core),
        )
        add_total(zh)

    def mixed_end(wave):
        arrive(zb.at[wave], z_recv.at[wave], z_send.at[wave])
        mixed_ref[wave * 256 : (wave + 1) * 256, :] = (
            total[wave, zh].astype(F32) + zb[wave].astype(F32)
        ).astype(BF16)

    parts_to_sibling(0)
    parts_to_sibling(1)
    for zz in range(4):
        start_back(*back(0, zz, query_piece(zz)))
    unpack(ol_ref, attn)
    terms_to_sibling(0)
    parts_far(0)
    terms_to_sibling(1)
    terms_far(0)
    parts_far(1)
    terms_far(1)
    parts_near(0)
    terms_near(0)
    parts_near(1)
    terms_near(1)
    parts_end(0)
    terms_end(0)
    parts_end(1)
    terms_end(1)
    mixed_end(0)
    mixed_end(1)
    for t in range(3):
        landed(t)
    for zz in range(4):
        sent_back(*back(0, zz, query_piece(zz)))
        for t in (0, 1):
            sent_back(*back(1 + t, zz, final.at[t, zz]))
    for copy in sent:
        copy.wait_send()


def scatter(ol, dq, dkv, w):
    vmem = pl.BlockSpec(memory_space=pltpu.VMEM)
    dma = pltpu.SemaphoreType.DMA
    return pl.pallas_call(
        scatter_kernel,
        out_shape=(
            jax.ShapeDtypeStruct((512, 256), BF16),
            jax.ShapeDtypeStruct((3, 2, 2, 2, BLOCK, HEAD_DIM), BF16),
        ),
        in_specs=[vmem] * 4,
        out_specs=(vmem,) * 2,
        scratch_shapes=[
            pltpu.VMEM((512, 256), BF16),
            pltpu.VMEM((2, 2, 4, 2, 256, 256), BF16),
            pltpu.VMEM((2, 4, 2, 256, 256), BF16),
            pltpu.VMEM((2, 2, 256, 256), BF16),
            pltpu.VMEM((2, 2, 2, 256, 256), BF16),
            pltpu.VMEM((2, 2, 256, 256), BF16),
            pltpu.VMEM((2, 256, 256), BF16),
            pltpu.VMEM((2, 4, 4, 2, BLOCK, HEAD_DIM), BF16),
            pltpu.VMEM((2, 4, 4, 2, BLOCK, HEAD_DIM), BF16),
            pltpu.VMEM((2, 2, 2, 2, BLOCK, HEAD_DIM), BF16),
            pltpu.VMEM((2, 2, 4, 2, BLOCK, HEAD_DIM), BF16),
            pltpu.VMEM((2, 4, 2, BLOCK, HEAD_DIM), BF16),
            dma((3, 4)),
            dma((3, 2, 2)),
            dma((2, 4)),
            dma((2, 4)),
            dma((2, 4)),
            dma((2, 4)),
            dma((2, 4)),
            dma((2, 4)),
            dma((2, 4)),
            dma((2, 4)),
            dma((2,)),
            dma((2,)),
        ],
        compiler_params=pltpu.CompilerParams(
            collective_id=1, has_side_effects=True, vmem_limit_bytes=VMEM_LIMIT
        ),
        name="scatter_heads",
    )(ol, dq, dkv, w)


def unpack_kernel(mixed_ref, lands_ref, mixed_out, dq_out, dk_out, dv_out):
    mixed_out[...] = mixed_ref[...]
    unpack(lands_ref.at[0], dq_out)
    unpack(lands_ref.at[1], dk_out)
    unpack(lands_ref.at[2], dv_out)


def unpack_all(mixed, lands):
    vmem = pl.BlockSpec(memory_space=pltpu.VMEM)
    return pl.pallas_call(
        unpack_kernel,
        out_shape=(jax.ShapeDtypeStruct((512, 256), BF16),) * 4,
        in_specs=[vmem] * 2,
        out_specs=(vmem,) * 4,
        name="unpack_outputs",
    )(mixed, lands)


def body(queries, keys, values, w_out, d_mixed, random_blocks, global_blocks):
    by_block = (4, BLOCK, 2 * HEAD_DIM)
    ids, q, da, probs, scores, dq, ol = gather(
        queries.reshape(by_block),
        keys.reshape(by_block),
        values.reshape(by_block),
        d_mixed,
        w_out,
        random_blocks,
        global_blocks,
    )
    dkv = key_grads(ids, q, da, probs, scores)
    dkv = dkv.reshape(4, 2, 2, 4, 2, BLOCK, HEAD_DIM)
    return unpack_all(*scatter(ol, dq, dkv, w_out))


def solution(mesh):
    return jax.shard_map(
        body,
        mesh=mesh,
        in_specs=(
            P("seq", "head"),
            P("seq", "head"),
            P("seq", "head"),
            P("head", None),
            P("seq", "head"),
            P("seq", None),
            P(),
        ),
        out_specs=(P("seq", "head"), P("seq", "head"), P("seq", "head"), P("seq", "head")),
        check_vma=False,
    )
```

time: 153 us -> 128 us (0.84); the launches traced: 151 us -> 128 us
  Pallas kernels: 143 us -> 127 us
  local copies, waits for them, and re-layouts: 7.95 us -> 0 us
    pallas_call x1, Pallas kernels: 58.6 us -> 48.5 us  [scatter(): pl.pallas_call(scatter_kernel, out_shape=(jax.ShapeDtypeStruct((512, 256)...]
    unnamed x4 -> x0, local copies, waits for them, and re-layouts: 6.68 us -> none
    pallas_call x2 -> x3, Pallas kernels: 84 us -> 78.8 us  [the longest x1 69.2 us: gather(): pl.pallas_call(gather_kernel, out_shape=(jax.ShapeDtypeStruct((4, 8, 128)...]
where the time goes in v2:
time: 128 us
  Pallas kernels  127 us (99%)
    pallas_call x1, Pallas kernels, gather(): pl.pallas_call(gather_kernel, out_shape=(jax.ShapeDtypeStruct((4, 8, 128)...  69.2 us
    pallas_call x1, Pallas kernels, scatter(): pl.pallas_call(scatter_kernel, out_shape=(jax.ShapeDtypeStruct((512, 256)...  48.5 us
    pallas_call x1, Pallas kernels, key_grads(): pl.pallas_call(key_grads_kernel, out_shape=jax.ShapeDtypeStruct((128, BLO...  7.29 us

profile of v2, /device:TPU:1, one launch (start us, length us, event | category | flops | bytes accessed | tf_op | source)
XLA Modules:
  0.0 127.9 jit_solution(8922851672818429692)
XLA Ops:
  0.6 69.2 %gather_heads.1 = (s32[4,8,128]{2,1,0:T(8,128)}, bf16[8,128,128]{2,1,0:T(8,128)(2,1)}, bf16[8,128,128]{2,1,0:T(8,128)(2,1)}, bf16[8,128,1024]{2,1,0:T(8,128)(2,1...) custom-call(bf16[4,128,256]{2,1,0:T(8,128)(2,1)} %bitcast.5, ...), custom_call_target="tpu_custom_call" | custom-call | tf_op jit(solution)/shard_map/gather_heads/pallas_call | solution.py:473
  69.9 7.3 %key_grads.1 = bf16[128,128,128]{2,1,0:T(8,128)(2,1)} custom-call(s32[4,8,128]{2,1,0:T(8,128)} %get-tuple-element.15.ids_ref, bf16[8,128,128]{2,1,0:T(8,128)(2,1)} %get-tuple-element.16.q_ref, bf16[8,128,128]{2,1,0:T(8,128)(2,1)} %get-tuple-element.17.da_ref, bf16[8,128,1024]{2,1,0:T(8,128)(2,1)} %get-tuple-element.18.probs_ref, ...), custom_call_target="tpu_custom_call" | custom-call | tf_op jit(solution)/shard_map/key_grads/pallas_call | solution.py:558
  77.2 48.5 %scatter_heads.1 = (bf16[512,256]{1,0:T(8,128)(2,1)}, bf16[3,2,2,2,128,128]{5,4,3,2,1,0:T(8,128)(2,1)}) custom-call(bf16[2,2,2,128,128]{4,3,2,1,0:T(8,128)(2,1)} %get-tuple-element.13.ol_ref, bf16[8,128,128]{2,1,0:T(8,128)(2,1)} %get-tuple-element.14.dq_ref, bf16[4,2,2,4,2,128,128]{6,5,4,3,2,1,0:T(8,128)(2,1)} %bitcast.4, bf16[256,4096]{1,0:T(8,128)(2,1)} %w_ref.3), custom_call_target="tpu_custom_call" | custom-call | tf_op jit(solution)/shard_map/scatter_heads/pallas_call | solution.py:830
  125.7 2.2 %unpack_outputs.1 = (bf16[512,256]{1,0:T(8,128)(2,1)}, bf16[512,256]{1,0:T(8,128)(2,1)}, bf16[512,256]{1,0:T(8,128)(2,1)}, bf16[512,256]{1,0:T(8,128)(2,1)}) custom-call(bf16[512,256]{1,0:T(8,128)(2,1)} %get-tuple-element.20.mixed_ref, bf16[3,2,2,2,128,128]{5,4,3,2,1,0:T(8,128)(2,1)} %get-tuple-element.21.lands_ref), custom_call_target="tpu_custom_call" | custom-call | tf_op jit(solution)/shard_map/unpack_outputs/pallas_call | solution.py:880

commit v3 on v2

--- a/solution.py
+++ b/solution.py
@@ -81,16 +81,19 @@
     k_ref,
     v_ref,
     dm_ref,
-    w_ref,
+    w_hbm,
     random_ref,
     global_ref,
     tables_ref,
     qm_ref,
     da_ref,
+    probs_hbm,
+    scores_hbm,
+    dq_ref,
+    ol_ref,
+    w_ref,
     probs_ref,
     scores_ref,
-    dq_ref,
-    ol_ref,
     kv_ref,
     table_ref,
     dm_all,
@@ -124,6 +127,8 @@
     z, y, x, zh, core = place()
     sibling = dev(z, y, x, zh, 1 - core)
     sent = []
+    load_w = pltpu.make_async_copy(w_hbm, w_ref, id_sem.at[1])
+    load_w.start()
     table_ref[...] = slot_table(random_ref, global_ref)
     greet()
 
@@ -354,6 +359,7 @@
     dm_from_far(0, 1)
     dm_from_ring(1, 1)
     kv_from_far(0)
+    load_w.wait()
     make_grad(0)
     dm_from_far(1, 1)
     kv_from_far(1)
@@ -399,7 +405,9 @@
         outs[n] = jnp.dot(half, vcat[n], preferred_element_type=F32).astype(BF16)
         return carry
 
-    lax.fori_loop(0, 8, forward, 0)
+    lax.fori_loop(0, 8, forward, 0, unroll=2)
+    keep_probs = pltpu.make_async_copy(probs_ref, probs_hbm, id_sem.at[2])
+    keep_probs.start()
 
     def out_here(zz):
         return jnp.logical_and(z == zz, z // 2 == core)
@@ -442,7 +450,9 @@
         dq_ref[n] = jnp.dot(score_grad, kcat[n], preferred_element_type=F32).astype(BF16)
         return carry
 
-    lax.fori_loop(0, 8, backward, 0)
+    lax.fori_loop(0, 8, backward, 0, unroll=2)
+    keep_scores = pltpu.make_async_copy(scores_ref, scores_hbm, id_sem.at[3])
+    keep_scores.start()
 
     for j in (0, 1):
         for r in (0, 1):
@@ -462,11 +472,14 @@
 
     for copy in sent:
         copy.wait_send()
+    keep_probs.wait()
+    keep_scores.wait()
 
 
 def gather(q, k, v, dm, w, random_blocks, global_blocks):
     vmem = pl.BlockSpec(memory_space=pltpu.VMEM)
     smem = pl.BlockSpec(memory_space=pltpu.SMEM)
+    hbm = pl.BlockSpec(memory_space=pl.ANY)
     dma = pltpu.SemaphoreType.DMA
     blocks = jax.ShapeDtypeStruct((8, BLOCK, HEAD_DIM), BF16)
     weights = jax.ShapeDtypeStruct((8, BLOCK, SLOTS * BLOCK), BF16)
@@ -481,9 +494,12 @@
             blocks,
             jax.ShapeDtypeStruct((2, 2, 2, BLOCK, HEAD_DIM), BF16),
         ),
-        in_specs=[vmem] * 5 + [smem] * 2,
-        out_specs=(vmem,) * 7,
+        in_specs=[vmem] * 4 + [hbm] + [smem] * 2,
+        out_specs=(vmem, vmem, vmem, hbm, hbm, vmem, vmem),
         scratch_shapes=[
+            pltpu.VMEM((256, 4096), BF16),
+            pltpu.VMEM((8, BLOCK, SLOTS * BLOCK), BF16),
+            pltpu.VMEM((8, BLOCK, SLOTS * BLOCK), BF16),
             pltpu.VMEM((128, BLOCK, HEAD_DIM), BF16),
             pltpu.VMEM((8, 128), jnp.int32),
             pltpu.VMEM((2, 2, 4, 2, 256, 256), BF16),
@@ -494,7 +510,7 @@
             pltpu.VMEM((8, BLOCK, SLOTS * BLOCK), F32),
             pltpu.VMEM((8, SLOTS * BLOCK, HEAD_DIM), BF16),
             pltpu.VMEM((8, SLOTS * BLOCK, HEAD_DIM), BF16),
-            dma((1,)),
+            dma((4,)),
             dma((3, 2, 2)),
             dma((3, 4)),
             dma((3,)),
@@ -521,8 +537,23 @@
     )(q, k, v, dm, w, random_blocks, global_blocks)
 
 
-def key_grads_kernel(ids_ref, q_ref, da_ref, probs_ref, scores_ref, dkv_ref, acc):
+def key_grads_kernel(
+    ids_ref, q_ref, da_ref, probs_hbm, scores_hbm, dkv_hbm, acc, probs_ref, scores_ref, half, sems, out_sems
+):
     core = place()[4]
+
+    def load(part):
+        rows = pl.ds(4 * part, 4)
+        return (
+            pltpu.make_async_copy(
+                scores_hbm.at[rows], scores_ref.at[rows], sems.at[part, 0]
+            ),
+            pltpu.make_async_copy(probs_hbm.at[rows], probs_ref.at[rows], sems.at[part, 1]),
+        )
+
+    for part in (0, 1):
+        for copy in load(part):
+            copy.start()
 
     def clear(i, carry):
         acc[i] = jnp.zeros((BLOCK, HEAD_DIM), F32)
@@ -543,24 +574,45 @@
             acc[at + 8] += value_add[t * BLOCK : (t + 1) * BLOCK, :]
         return carry
 
-    lax.fori_loop(0, 8, one, 0, unroll=2)
-
-    def finish(i, carry):
-        dkv_ref[i] = acc[i].astype(BF16)
-        return carry
-
-    lax.fori_loop(0, 128, finish, 0, unroll=8)
+    for part in (0, 1):
+        for copy in load(part):
+            copy.wait()
+        lax.fori_loop(4 * part, 4 * part + 4, one, 0, unroll=2)
+
+    def store(part):
+        rows = pl.ds(16 * part, 16)
+        return pltpu.make_async_copy(half.at[rows], dkv_hbm.at[rows], out_sems.at[part])
+
+    for part in range(8):
+
+        def finish(i, carry):
+            half[i] = acc[i].astype(BF16)
+            return carry
+
+        lax.fori_loop(16 * part, 16 * part + 16, finish, 0, unroll=8)
+        store(part).start()
+    for part in range(8):
+        store(part).wait()
 
 
 def key_grads(ids, q, da, probs, scores):
     vmem = pl.BlockSpec(memory_space=pltpu.VMEM)
     smem = pl.BlockSpec(memory_space=pltpu.SMEM)
+    hbm = pl.BlockSpec(memory_space=pl.ANY)
+    dma = pltpu.SemaphoreType.DMA
     return pl.pallas_call(
         key_grads_kernel,
         out_shape=jax.ShapeDtypeStruct((128, BLOCK, HEAD_DIM), BF16),
-        in_specs=[smem, vmem, vmem, vmem, vmem],
-        out_specs=vmem,
-        scratch_shapes=[pltpu.VMEM((128, BLOCK, HEAD_DIM), F32)],
+        in_specs=[smem, vmem, vmem, hbm, hbm],
+        out_specs=hbm,
+        scratch_shapes=[
+            pltpu.VMEM((128, BLOCK, HEAD_DIM), F32),
+            pltpu.VMEM((8, BLOCK, SLOTS * BLOCK), BF16),
+            pltpu.VMEM((8, BLOCK, SLOTS * BLOCK), BF16),
+            pltpu.VMEM((128, BLOCK, HEAD_DIM), BF16),
+            dma((2, 2)),
+            dma((8,)),
+        ],
         compiler_params=pltpu.CompilerParams(vmem_limit_bytes=VMEM_LIMIT),
         name="key_grads",
     )(ids, q, da, probs, scores)
@@ -577,10 +629,13 @@
 def scatter_kernel(
     ol_ref,
     dq_ref,
-    p_ref,
-    w_ref,
+    p_hbm,
+    w_hbm,
     mixed_ref,
     lands,
+    w_ref,
+    p_ref,
+    load_sems,
     attn,
     terms,
     terms_in,
@@ -609,6 +664,11 @@
     z, y, x, zh, core = place()
     sibling = dev(z, y, x, zh, 1 - core)
     sent = []
+    load_w = pltpu.make_async_copy(w_hbm, w_ref, load_sems.at[0])
+    load_p = pltpu.make_async_copy(p_hbm.at[:, core], p_ref, load_sems.at[1])
+    load_w.start()
+    load_p.start()
+    unpack(ol_ref, attn)
     greet()
 
     def send(src, dst, send_sem, recv_sem, device):
@@ -657,7 +717,7 @@
     def parts_to_sibling(t):
         for n in range(4):
             send(
-                p_ref.at[y_of[n], 1 - core, t],
+                p_hbm.at[y_of[n], 1 - core, t],
                 parts_in.at[t, n],
                 ps_send.at[t, n],
                 ps_recv.at[t, n],
@@ -665,7 +725,7 @@
             )
 
     def add_parts(t, n, zz, more):
-        value = p_ref[y_of[n], core, t, zz].astype(F32) + parts_in[t, n, zz].astype(F32)
+        value = p_ref[y_of[n], t, zz].astype(F32) + parts_in[t, n, zz].astype(F32)
         for ref in more:
             value += ref.astype(F32)
         return value.astype(BF16)
@@ -797,8 +857,9 @@
     parts_to_sibling(1)
     for zz in range(4):
         start_back(*back(0, zz, query_piece(zz)))
-    unpack(ol_ref, attn)
+    load_w.wait()
     terms_to_sibling(0)
+    load_p.wait()
     parts_far(0)
     terms_to_sibling(1)
     terms_far(0)
@@ -826,6 +887,7 @@
 
 def scatter(ol, dq, dkv, w):
     vmem = pl.BlockSpec(memory_space=pltpu.VMEM)
+    hbm = pl.BlockSpec(memory_space=pl.ANY)
     dma = pltpu.SemaphoreType.DMA
     return pl.pallas_call(
         scatter_kernel,
@@ -833,9 +895,12 @@
             jax.ShapeDtypeStruct((512, 256), BF16),
             jax.ShapeDtypeStruct((3, 2, 2, 2, BLOCK, HEAD_DIM), BF16),
         ),
-        in_specs=[vmem] * 4,
+        in_specs=[vmem, vmem, hbm, hbm],
         out_specs=(vmem,) * 2,
         scratch_shapes=[
+            pltpu.VMEM((256, 4096), BF16),
+            pltpu.VMEM((4, 2, 4, 2, BLOCK, HEAD_DIM), BF16),
+            dma((2,)),
             pltpu.VMEM((512, 256), BF16),
             pltpu.VMEM((2, 2, 4, 2, 256, 256), BF16),
             pltpu.VMEM((2, 4, 2, 256, 256), BF16),

time: 128 us -> 122 us (0.953)
  Pallas kernels: 127 us -> 121 us
    pallas_call x1, Pallas kernels: 48.5 us -> 45.5 us  [scatter(): pl.pallas_call(scatter_kernel, out_shape=(jax.ShapeDtypeStruct((512, 256)...]
    pallas_call x1, Pallas kernels: 69.2 us -> 66.6 us  [gather(): pl.pallas_call(gather_kernel, out_shape=(jax.ShapeDtypeStruct((4, 8, 128)...]
where the time goes in v3:
time: 122 us
  Pallas kernels  121 us (99%)
    pallas_call x1, Pallas kernels, gather(): pl.pallas_call(gather_kernel, out_shape=(jax.ShapeDtypeStruct((4, 8, 128)...  66.6 us
    pallas_call x1, Pallas kernels, scatter(): pl.pallas_call(scatter_kernel, out_shape=(jax.ShapeDtypeStruct((512, 256)...  45.5 us
    pallas_call x1, Pallas kernels, key_grads(): pl.pallas_call(key_grads_kernel, out_shape=jax.ShapeDtypeStruct((128, BLO...  6.57 us

profile of v3, /device:TPU:1, one launch (start us, length us, event | category | flops | bytes accessed | tf_op | source)
XLA Modules:
  0.0 121.6 jit_solution(14718833363525741985)
XLA Ops:
  0.6 66.6 %gather_heads.1 = (s32[4,8,128]{2,1,0:T(8,128)}, bf16[8,128,128]{2,1,0:T(8,128)(2,1)}, bf16[8,128,128]{2,1,0:T(8,128)(2,1)}, bf16[8,128,1024]{2,1,0:T(8,128)(2,1...) custom-call(bf16[4,128,256]{2,1,0:T(8,128)(2,1)} %bitcast.5, ...), custom_call_target="tpu_custom_call" | custom-call | tf_op jit(solution)/shard_map/gather_heads/pallas_call | solution.py:486
  67.3 6.6 %key_grads.1 = bf16[128,128,128]{2,1,0:T(8,128)(2,1)} custom-call(s32[4,8,128]{2,1,0:T(8,128)} %get-tuple-element.15.ids_ref, bf16[8,128,128]{2,1,0:T(8,128)(2,1)} %get-tuple-element.16.q_ref, bf16[8,128,128]{2,1,0:T(8,128)(2,1)} %get-tuple-element.17.da_ref, bf16[8,128,1024]{2,1,0:T(8,128)(2,1)} %get-tuple-element.18.probs_hbm, ...), custom_call_target="tpu_custom_call" | custom-call | tf_op jit(solution)/shard_map/key_grads/pallas_call | solution.py:603
  73.8 45.5 %scatter_heads.1 = (bf16[512,256]{1,0:T(8,128)(2,1)}, bf16[3,2,2,2,128,128]{5,4,3,2,1,0:T(8,128)(2,1)}) custom-call(bf16[2,2,2,128,128]{4,3,2,1,0:T(8,128)(2,1)} %get-tuple-element.13.ol_ref, bf16[8,128,128]{2,1,0:T(8,128)(2,1)} %get-tuple-element.14.dq_ref, bf16[4,2,2,4,2,128,128]{6,5,4,3,2,1,0:T(8,128)(2,1)} %bitcast.4, bf16[256,4096]{1,0:T(8,128)(2,1)} %w_hbm.3), custom_call_target="tpu_custom_call" | custom-call | tf_op jit(solution)/shard_map/scatter_heads/pallas_call | solution.py:892
  119.3 2.2 %unpack_outputs.1 = (bf16[512,256]{1,0:T(8,128)(2,1)}, bf16[512,256]{1,0:T(8,128)(2,1)}, bf16[512,256]{1,0:T(8,128)(2,1)}, bf16[512,256]{1,0:T(8,128)(2,1)}) custom-call(bf16[512,256]{1,0:T(8,128)(2,1)} %get-tuple-element.20.mixed_ref, bf16[3,2,2,2,128,128]{5,4,3,2,1,0:T(8,128)(2,1)} %get-tuple-element.21.lands_ref), custom_call_target="tpu_custom_call" | custom-call | tf_op jit(solution)/shard_map/unpack_outputs/pallas_call | solution.py:945

commit v4 on v3

--- a/solution.py
+++ b/solution.py
@@ -306,7 +306,7 @@
             )
             return carry
 
-        lax.fori_loop(0, 8, step, 0)
+        lax.fori_loop(0, 8, step, 0, unroll=True)
 
     def make_grad(wave):
         add_product(wave, core, True)
@@ -405,7 +405,7 @@
         outs[n] = jnp.dot(half, vcat[n], preferred_element_type=F32).astype(BF16)
         return carry
 
-    lax.fori_loop(0, 8, forward, 0, unroll=2)
+    lax.fori_loop(0, 8, forward, 0, unroll=4)
     keep_probs = pltpu.make_async_copy(probs_ref, probs_hbm, id_sem.at[2])
     keep_probs.start()
 
@@ -450,7 +450,7 @@
         dq_ref[n] = jnp.dot(score_grad, kcat[n], preferred_element_type=F32).astype(BF16)
         return carry
 
-    lax.fori_loop(0, 8, backward, 0, unroll=2)
+    lax.fori_loop(0, 8, backward, 0, unroll=4)
     keep_scores = pltpu.make_async_copy(scores_ref, scores_hbm, id_sem.at[3])
     keep_scores.start()
 
@@ -684,9 +684,9 @@
     y_of = ((y + 2) % 4, (y + 1) % 4, (y + 3) % 4, y)
     x_of = ((x + 2) % 4, (x + 1) % 4, (x + 3) % 4, x)
 
-    def back(t, zz, src):
-        dst = lands.at[t, z % 2, core]
-        return src, dst, l_send.at[t, zz], l_recv.at[t, z % 2, core], zz
+    def back(u, zz, src):
+        dst = lands.at[0, z % 2, core] if u == 0 else grad_land(u - 1, z % 2, core)
+        return src, dst, l_send.at[u, zz], l_recv.at[u, z % 2, core], zz
 
     def start_back(src, dst, send_sem, recv_sem, zz):
         here = jnp.logical_and(z == zz, z // 2 == core)
@@ -706,10 +706,14 @@
         def _():
             copy_to(src, dst, send_sem, recv_sem, dev(zz, y, x, zh, z // 2)).wait_send()
 
-    def landed(t):
+    def landed(u):
         for j in (0, 1):
             for r in (0, 1):
-                arrive(lands.at[t, j, r], l_recv.at[t, j, r], l_send.at[t, 0])
+                dst = lands.at[0, j, r] if u == 0 else grad_land(u - 1, j, r)
+                arrive(dst, l_recv.at[u, j, r], l_send.at[u, 0])
+
+    def grad_land(u, j, r):
+        return lands.at[1 + u // 2, j, r, u % 2]
 
     def query_piece(zz):
         return dq_ref.at[pl.ds(2 * zz, 2)]
@@ -717,7 +721,7 @@
     def parts_to_sibling(t):
         for n in range(4):
             send(
-                p_hbm.at[y_of[n], 1 - core, t],
+                p_hbm.at[y_of[n], 1 - core, t // 2, :, t % 2],
                 parts_in.at[t, n],
                 ps_send.at[t, n],
                 ps_recv.at[t, n],
@@ -725,7 +729,7 @@
             )
 
     def add_parts(t, n, zz, more):
-        value = p_ref[y_of[n], t, zz].astype(F32) + parts_in[t, n, zz].astype(F32)
+        value = p_ref[y_of[n], t // 2, zz, t % 2].astype(F32) + parts_in[t, n, zz].astype(F32)
         for ref in more:
             value += ref.astype(F32)
         return value.astype(BF16)
@@ -776,7 +780,7 @@
         for k in (0, 1):
             at = pl.multiple_of((x_of[n] * 4 + k * 2 + to_core) * 256, 256)
             terms[wave, to_core, n, k] = jnp.dot(
-                attn[wave * 256 : (wave + 1) * 256, :],
+                attn[wave * 128 : (wave + 1) * 128, :],
                 w_ref[:, pl.ds(at, 256)],
                 preferred_element_type=F32,
             ).astype(BF16)
@@ -849,7 +853,7 @@
 
     def mixed_end(wave):
         arrive(zb.at[wave], z_recv.at[wave], z_send.at[wave])
-        mixed_ref[wave * 256 : (wave + 1) * 256, :] = (
+        mixed_ref[wave * 128 : (wave + 1) * 128, :] = (
             total[wave, zh].astype(F32) + zb[wave].astype(F32)
         ).astype(BF16)
 
@@ -861,25 +865,41 @@
     terms_to_sibling(0)
     load_p.wait()
     parts_far(0)
+    parts_to_sibling(2)
     terms_to_sibling(1)
     terms_far(0)
     parts_far(1)
+    parts_to_sibling(3)
+    terms_to_sibling(2)
+    parts_near(0)
     terms_far(1)
-    parts_near(0)
+    parts_far(2)
+    terms_to_sibling(3)
     terms_near(0)
     parts_near(1)
+    terms_far(2)
+    parts_far(3)
+    parts_end(0)
     terms_near(1)
-    parts_end(0)
+    parts_near(2)
+    terms_far(3)
     terms_end(0)
     parts_end(1)
+    terms_near(2)
+    parts_near(3)
     terms_end(1)
-    mixed_end(0)
-    mixed_end(1)
-    for t in range(3):
-        landed(t)
+    parts_end(2)
+    terms_near(3)
+    terms_end(2)
+    parts_end(3)
+    terms_end(3)
+    for wave in range(4):
+        mixed_end(wave)
+    for u in range(5):
+        landed(u)
     for zz in range(4):
         sent_back(*back(0, zz, query_piece(zz)))
-        for t in (0, 1):
+        for t in range(4):
             sent_back(*back(1 + t, zz, final.at[t, zz]))
     for copy in sent:
         copy.wait_send()
@@ -902,29 +922,29 @@
             pltpu.VMEM((4, 2, 4, 2, BLOCK, HEAD_DIM), BF16),
             dma((2,)),
             pltpu.VMEM((512, 256), BF16),
-            pltpu.VMEM((2, 2, 4, 2, 256, 256), BF16),
-            pltpu.VMEM((2, 4, 2, 256, 256), BF16),
-            pltpu.VMEM((2, 2, 256, 256), BF16),
-            pltpu.VMEM((2, 2, 2, 256, 256), BF16),
-            pltpu.VMEM((2, 2, 256, 256), BF16),
-            pltpu.VMEM((2, 256, 256), BF16),
-            pltpu.VMEM((2, 4, 4, 2, BLOCK, HEAD_DIM), BF16),
-            pltpu.VMEM((2, 4, 4, 2, BLOCK, HEAD_DIM), BF16),
-            pltpu.VMEM((2, 2, 2, 2, BLOCK, HEAD_DIM), BF16),
-            pltpu.VMEM((2, 2, 4, 2, BLOCK, HEAD_DIM), BF16),
-            pltpu.VMEM((2, 4, 2, BLOCK, HEAD_DIM), BF16),
-            dma((3, 4)),
-            dma((3, 2, 2)),
-            dma((2, 4)),
-            dma((2, 4)),
-            dma((2, 4)),
-            dma((2, 4)),
-            dma((2, 4)),
-            dma((2, 4)),
-            dma((2, 4)),
-            dma((2, 4)),
-            dma((2,)),
-            dma((2,)),
+            pltpu.VMEM((4, 2, 4, 2, 128, 256), BF16),
+            pltpu.VMEM((4, 4, 2, 128, 256), BF16),
+            pltpu.VMEM((4, 2, 128, 256), BF16),
+            pltpu.VMEM((4, 2, 2, 128, 256), BF16),
+            pltpu.VMEM((4, 2, 128, 256), BF16),
+            pltpu.VMEM((4, 128, 256), BF16),
+            pltpu.VMEM((4, 4, 4, BLOCK, HEAD_DIM), BF16),
+            pltpu.VMEM((4, 4, 4, BLOCK, HEAD_DIM), BF16),
+            pltpu.VMEM((4, 2, 2, BLOCK, HEAD_DIM), BF16),
+            pltpu.VMEM((4, 2, 4, BLOCK, HEAD_DIM), BF16),
+            pltpu.VMEM((4, 4, BLOCK, HEAD_DIM), BF16),
+            dma((5, 4)),
+            dma((5, 2, 2)),
+            dma((4, 4)),
+            dma((4, 4)),
+            dma((4, 4)),
+            dma((4, 4)),
+            dma((4, 4)),
+            dma((4, 4)),
+            dma((4, 4)),
+            dma((4, 4)),
+            dma((4,)),
+            dma((4,)),
         ],
         compiler_params=pltpu.CompilerParams(
             collective_id=1, has_side_effects=True, vmem_limit_bytes=VMEM_LIMIT

time: 122 us -> 117 us (0.959)
  Pallas kernels: 121 us -> 116 us
    pallas_call x1, Pallas kernels: 66.6 us -> 63.9 us  [gather(): pl.pallas_call(gather_kernel, out_shape=(jax.ShapeDtypeStruct((4, 8, 128)...]
    pallas_call x1, Pallas kernels: 45.5 us -> 43.6 us  [scatter(): pl.pallas_call(scatter_kernel, out_shape=(jax.ShapeDtypeStruct((512, 256)...]
where the time goes in v4:
time: 117 us
  Pallas kernels  116 us (99%)
    pallas_call x1, Pallas kernels, gather(): pl.pallas_call(gather_kernel, out_shape=(jax.ShapeDtypeStruct((4, 8, 128)...  63.9 us
    pallas_call x1, Pallas kernels, scatter(): pl.pallas_call(scatter_kernel, out_shape=(jax.ShapeDtypeStruct((512, 256)...  43.6 us
    pallas_call x1, Pallas kernels, key_grads(): pl.pallas_call(key_grads_kernel, out_shape=jax.ShapeDtypeStruct((128, BLO...  6.57 us

profile of v4, /device:TPU:1, one launch (start us, length us, event | category | flops | bytes accessed | tf_op | source)
XLA Modules:
  0.0 116.9 jit_solution(7704785852101004974)
XLA Ops:
  0.6 63.9 %gather_heads.1 = (s32[4,8,128]{2,1,0:T(8,128)}, bf16[8,128,128]{2,1,0:T(8,128)(2,1)}, bf16[8,128,128]{2,1,0:T(8,128)(2,1)}, bf16[8,128,1024]{2,1,0:T(8,128)(2,1...) custom-call(bf16[4,128,256]{2,1,0:T(8,128)(2,1)} %bitcast.5, ...), custom_call_target="tpu_custom_call" | custom-call | tf_op jit(solution)/shard_map/gather_heads/pallas_call | solution.py:486
  64.5 6.6 %key_grads.1 = bf16[128,128,128]{2,1,0:T(8,128)(2,1)} custom-call(s32[4,8,128]{2,1,0:T(8,128)} %get-tuple-element.15.ids_ref, bf16[8,128,128]{2,1,0:T(8,128)(2,1)} %get-tuple-element.16.q_ref, bf16[8,128,128]{2,1,0:T(8,128)(2,1)} %get-tuple-element.17.da_ref, bf16[8,128,1024]{2,1,0:T(8,128)(2,1)} %get-tuple-element.18.probs_hbm, ...), custom_call_target="tpu_custom_call" | custom-call | tf_op jit(solution)/shard_map/key_grads/pallas_call | solution.py:603
  71.1 43.6 %scatter_heads.1 = (bf16[512,256]{1,0:T(8,128)(2,1)}, bf16[3,2,2,2,128,128]{5,4,3,2,1,0:T(8,128)(2,1)}) custom-call(bf16[2,2,2,128,128]{4,3,2,1,0:T(8,128)(2,1)} %get-tuple-element.13.ol_ref, bf16[8,128,128]{2,1,0:T(8,128)(2,1)} %get-tuple-element.14.dq_ref, bf16[4,2,2,4,2,128,128]{6,5,4,3,2,1,0:T(8,128)(2,1)} %bitcast.4, bf16[256,4096]{1,0:T(8,128)(2,1)} %w_hbm.3), custom_call_target="tpu_custom_call" | custom-call | tf_op jit(solution)/shard_map/scatter_heads/pallas_call | solution.py:912
  114.7 2.2 %unpack_outputs.1 = (bf16[512,256]{1,0:T(8,128)(2,1)}, bf16[512,256]{1,0:T(8,128)(2,1)}, bf16[512,256]{1,0:T(8,128)(2,1)}, bf16[512,256]{1,0:T(8,128)(2,1)}) custom-call(bf16[512,256]{1,0:T(8,128)(2,1)} %get-tuple-element.20.mixed_ref, bf16[3,2,2,2,128,128]{5,4,3,2,1,0:T(8,128)(2,1)} %get-tuple-element.21.lands_ref), custom_call_target="tpu_custom_call" | custom-call | tf_op jit(solution)/shard_map/unpack_outputs/pallas_call | solution.py:965

commit v5 on v4

--- a/solution.py
+++ b/solution.py
@@ -323,14 +323,14 @@
         for args in grad_args(wave):
             to_line(*args)
 
+    dm_to_partner(0)
     for args in kv_args(0):
         to_line(*args)
-    dm_to_partner(0)
     for wave in (0, 1):
         dm_to_ring(wave, 0, own_rows(wave))
+    dm_to_partner(1)
     for args in kv_args(1):
         to_line(*args)
-    dm_to_partner(1)
     for step in (1, 2, 3):
         send(
             table_ref,
@@ -405,10 +405,6 @@
         outs[n] = jnp.dot(half, vcat[n], preferred_element_type=F32).astype(BF16)
         return carry
 
-    lax.fori_loop(0, 8, forward, 0, unroll=4)
-    keep_probs = pltpu.make_async_copy(probs_ref, probs_hbm, id_sem.at[2])
-    keep_probs.start()
-
     def out_here(zz):
         return jnp.logical_and(z == zz, z // 2 == core)
 
@@ -425,6 +421,8 @@
         )
 
     for zz in range(4):
+        if zz % 2 == 0:
+            lax.fori_loop(2 * zz, 2 * zz + 4, forward, 0, unroll=4)
 
         @pl.when(out_here(zz))
         def _():
@@ -436,8 +434,8 @@
         def _():
             out_copy(zz).start()
 
-    for zz in range(4):
-        arrive(da_ref.at[pl.ds(2 * zz, 2)], g_recv.at[zz], g_send.at[0, 0])
+    keep_probs = pltpu.make_async_copy(probs_ref, probs_hbm, id_sem.at[2])
+    keep_probs.start()
 
     def backward(n, carry):
         grad_rows = da_ref[n]
@@ -450,7 +448,10 @@
         dq_ref[n] = jnp.dot(score_grad, kcat[n], preferred_element_type=F32).astype(BF16)
         return carry
 
-    lax.fori_loop(0, 8, backward, 0, unroll=4)
+    for zz in range(4):
+        arrive(da_ref.at[pl.ds(2 * zz, 2)], g_recv.at[zz], g_send.at[0, 0])
+        if zz % 2 == 1:
+            lax.fori_loop(2 * zz - 2, 2 * zz + 2, backward, 0, unroll=4)
     keep_scores = pltpu.make_async_copy(scores_ref, scores_hbm, id_sem.at[3])
     keep_scores.start()
 

time: 117 us -> 116 us (level)
    pallas_call x1, Pallas kernels: 63.9 us -> 62.1 us  [gather(): pl.pallas_call(gather_kernel, out_shape=(jax.ShapeDtypeStruct((4, 8, 128)...]
where the time goes in v5:
time: 116 us
  Pallas kernels  115 us (99%)
    pallas_call x1, Pallas kernels, gather(): pl.pallas_call(gather_kernel, out_shape=(jax.ShapeDtypeStruct((4, 8, 128)...  62.1 us
    pallas_call x1, Pallas kernels, scatter(): pl.pallas_call(scatter_kernel, out_shape=(jax.ShapeDtypeStruct((512, 256)...  44.3 us
    pallas_call x1, Pallas kernels, key_grads(): pl.pallas_call(key_grads_kernel, out_shape=jax.ShapeDtypeStruct((128, BLO...  6.57 us

profile of v5, /device:TPU:1, one launch (start us, length us, event | category | flops | bytes accessed | tf_op | source)
XLA Modules:
  0.0 115.9 jit_solution(2451248602396598030)
XLA Ops:
  0.6 62.1 %gather_heads.1 = (s32[4,8,128]{2,1,0:T(8,128)}, bf16[8,128,128]{2,1,0:T(8,128)(2,1)}, bf16[8,128,128]{2,1,0:T(8,128)(2,1)}, bf16[8,128,1024]{2,1,0:T(8,128)(2,1...) custom-call(bf16[4,128,256]{2,1,0:T(8,128)(2,1)} %bitcast.5, ...), custom_call_target="tpu_custom_call" | custom-call | tf_op jit(solution)/shard_map/gather_heads/pallas_call | solution.py:487
  62.7 6.6 %key_grads.1 = bf16[128,128,128]{2,1,0:T(8,128)(2,1)} custom-call(s32[4,8,128]{2,1,0:T(8,128)} %get-tuple-element.15.ids_ref, bf16[8,128,128]{2,1,0:T(8,128)(2,1)} %get-tuple-element.16.q_ref, bf16[8,128,128]{2,1,0:T(8,128)(2,1)} %get-tuple-element.17.da_ref, bf16[8,128,1024]{2,1,0:T(8,128)(2,1)} %get-tuple-element.18.probs_hbm, ...), custom_call_target="tpu_custom_call" | custom-call | tf_op jit(solution)/shard_map/key_grads/pallas_call | solution.py:604
  69.3 44.3 %scatter_heads.1 = (bf16[512,256]{1,0:T(8,128)(2,1)}, bf16[3,2,2,2,128,128]{5,4,3,2,1,0:T(8,128)(2,1)}) custom-call(bf16[2,2,2,128,128]{4,3,2,1,0:T(8,128)(2,1)} %get-tuple-element.13.ol_ref, bf16[8,128,128]{2,1,0:T(8,128)(2,1)} %get-tuple-element.14.dq_ref, bf16[4,2,2,4,2,128,128]{6,5,4,3,2,1,0:T(8,128)(2,1)} %bitcast.4, bf16[256,4096]{1,0:T(8,128)(2,1)} %w_hbm.3), custom_call_target="tpu_custom_call" | custom-call | tf_op jit(solution)/shard_map/scatter_heads/pallas_call | solution.py:913
  113.7 2.2 %unpack_outputs.1 = (bf16[512,256]{1,0:T(8,128)(2,1)}, bf16[512,256]{1,0:T(8,128)(2,1)}, bf16[512,256]{1,0:T(8,128)(2,1)}, bf16[512,256]{1,0:T(8,128)(2,1)}) custom-call(bf16[512,256]{1,0:T(8,128)(2,1)} %get-tuple-element.20.mixed_ref, bf16[3,2,2,2,128,128]{5,4,3,2,1,0:T(8,128)(2,1)} %get-tuple-element.21.lands_ref), custom_call_target="tpu_custom_call" | custom-call | tf_op jit(solution)/shard_map/unpack_outputs/pallas_call | solution.py:966
